TPU v7x, 128 devices: a whole 4x4x4 slice. The times are simulated.
128 devices in a mesh: ctx: 16 (over z, y), mp: 8 (over x, core).
Axes of the slice: x: 4, y: 4, z: 4, core: 2. Of those that a mesh axis runs over, the one named last changes fastest.
Arguments:
- ssd_x: bfloat16 [4096, 16384], P('ctx', 'mp'), may hold values from -6 to 6
- ssd_b: bfloat16 [4096, 128], P('ctx'), may hold values from -0.80078125 to 0.80078125
- ssd_c: bfloat16 [4096, 128], P('ctx'), may hold values from -0.80078125 to 0.80078125
- dt_steps: float32 [64, 4096], P('mp', 'ctx'), may hold values from 0 to 0.6, as said below
- decay_rate: float32 [64], P('mp'), may hold values from 0.5 to 2
- skip_gain: float32 [64], P('mp'), may hold values from 0.5 to 1.5
- doc_ids: int32 [4096], P('ctx'), may hold values from 0 to 3, never falling along the last dimension, each value on 1 to 2048 neighbouring positions
- queries: bfloat16 [4096, 8192], P('ctx', 'mp'), may hold values from -4.5 to 4.5
- key_rows: bfloat16 [4096, 1024], P('ctx', 'mp'), may hold values from -4.5 to 4.5
- values: bfloat16 [4096, 1024], P('ctx', 'mp'), may hold values from -6 to 6
- log_scale: float32 [64], P('mp'), may hold values from 0.05 to 0.15
- moe_in: bfloat16 [4096, 8192], P('ctx', 'mp'), may hold values from -6 to 6
- expert_ids: int32 [4096, 2], P('ctx'), may hold values from 0 to 15, as said below
- route_weights: float32 [4096, 2], P('ctx'), may hold values from 0.1 to 0.9
- w_gate: bfloat16 [8, 8192, 6144], P('mp', None, 'ctx'), may hold values from -0.0625 to 0.0625
- w_up: bfloat16 [8, 8192, 6144], P('mp', None, 'ctx'), may hold values from -0.0625 to 0.0625
- w_down: bfloat16 [8, 6144, 8192], P('mp', 'ctx'), may hold values from -0.0546875 to 0.0546875
Outputs:
- ssd_out: bfloat16 [4096, 16384], P('ctx', 'mp')
- attn_out: bfloat16 [4096, 8192], P('ctx', 'mp')
- moe_out: bfloat16 [4096, 8192], P('ctx', 'mp')
Inputs may be any that keep to these rules, and one draw needn't show every extreme that they name: `dt_steps`: Positive. `expert_ids`: each row names two different experts. In every aligned block of 256 rows (the tokens of one index of ctx) each of the 16 experts is named by exactly 32 rows, and the experts fall into two sets of 8 such that every row of the block names one of each set.
All inputs are finite; a program needn't handle non-finite values.
Results may differ from a plain program's by a relative error of at most 0.02.
Values may be sent and summed in bfloat16 or wider, within the bound.
A program may use at most 128 MiB of HBM per device.

v0:
```python
import math

import jax
import jax.numpy as jnp
from jax import lax
from jax.sharding import PartitionSpec as P

HEAD_DIM = 128
EXPERTS = 16
HELD = 4
SEG = 128


def prefix(array, axis, combine, identity):
    count, mine = (lax.axis_size(axis), lax.axis_index(axis))
    everything = jax.tree.map(
        lambda part, kind: lax.all_gather(part.astype(kind), axis),
        array,
        jax.tree.map(lambda a: jnp.bfloat16 if a.dtype == jnp.float32 else a.dtype, array),
    )
    start = jax.tree.map(
        lambda part, zero: jnp.broadcast_to(jnp.asarray(zero, part.dtype), part.shape),
        array,
        identity,
    )

    def lap(k, before):
        reached = k < mine
        new = combine(
            before, jax.tree.map(lambda part, own: part[k].astype(own.dtype), everything, array)
        )
        return jax.tree.map(lambda a, b: jnp.where(reached, a, b), new, before)

    return lax.fori_loop(0, count, lap, start)


def join(earlier, later):
    decay_early, state_early, first_early, last_early = earlier
    decay_late, state_late, first_late, last_late = later
    linked = jnp.where(
        (last_early < 0) | (first_late < 0), 1.0, (last_early == first_late).astype(jnp.float32)
    )
    decay_total = decay_early * decay_late * linked
    state_total = state_late + (decay_late * linked)[:, None, None] * state_early
    first_total = jnp.where(first_early < 0, first_late, first_early)
    last_total = jnp.where(last_late < 0, last_early, last_late)
    return (decay_total, state_total, first_total, last_total)


def ssd_layer(ssd_x, ssd_b, ssd_c, dt_steps, decay_rate, skip_gain, doc_ids):
    positions = ssd_x.shape[0]
    head_count = skip_gain.shape[0]
    attention_dimension = ssd_x.shape[1] // head_count
    state_count = ssd_b.shape[1]
    blocks = positions // SEG
    x_blocks = ssd_x.reshape(blocks, SEG, head_count, attention_dimension)
    b_blocks = ssd_b.reshape(blocks, SEG, state_count)
    c_blocks = ssd_c.reshape(blocks, SEG, state_count)
    doc_blocks = doc_ids.reshape(blocks, SEG)
    log_decay = -(dt_steps * decay_rate[:, None])
    cumulative = jnp.cumsum(log_decay.reshape(head_count, blocks, SEG), axis=2).transpose(1, 0, 2)
    causal = jnp.arange(SEG)[:, None] >= jnp.arange(SEG)[None, :]
    linked = (doc_blocks[:, :, None] == doc_blocks[:, None, :]) & causal[None]
    inner_prod = jnp.einsum("ktn,ksn->kts", c_blocks, b_blocks, preferred_element_type=jnp.float32)
    decay_gaps = cumulative[:, :, :, None] - cumulative[:, :, None, :]
    decay_mask = jnp.where(
        linked[:, None], jnp.exp(jnp.where(linked[:, None], decay_gaps, 0.0)), 0.0
    )
    weights = (inner_prod[:, None] * decay_mask).astype(jnp.bfloat16)
    block_term = jnp.einsum(
        "khts,kshp->kthp", weights, x_blocks, preferred_element_type=jnp.float32
    )
    first_docs = doc_blocks[:, 0]
    end_docs = doc_blocks[:, -1]
    tail_fade = jnp.where(
        doc_blocks[:, None, :] == end_docs[:, None, None],
        jnp.exp(cumulative[:, :, -1:] - cumulative),
        0.0,
    )
    scaled = (x_blocks * jnp.transpose(tail_fade, (0, 2, 1))[..., None]).astype(jnp.bfloat16)
    local_state = jnp.einsum("kshp,ksn->khpn", scaled, b_blocks, preferred_element_type=jnp.float32)
    block_decay = (
        jnp.exp(cumulative[:, :, -1]) * (first_docs == end_docs).astype(jnp.float32)[:, None]
    )
    first_float = first_docs.astype(jnp.float32)[:, None]
    end_float = end_docs.astype(jnp.float32)[:, None]
    identity = (
        jnp.ones((head_count,), jnp.float32),
        jnp.zeros((head_count, attention_dimension, state_count), jnp.float32),
        jnp.full((1,), -1.0, jnp.float32),
        jnp.full((1,), -1.0, jnp.float32),
    )

    def summarize(running, block_item):
        return (join(running, block_item), None)

    summary, unused = lax.scan(
        summarize, identity, (block_decay, local_state, first_float, end_float)
    )
    before = prefix(summary, "ctx", join, identity)

    def advance(running, block_item):
        carried_state, last_doc = running
        decay_here, local_here, first_here, end_here = block_item
        carried_flag = (last_doc == first_here).astype(jnp.float32)
        entering = carried_state * carried_flag
        return ((decay_here[:, None, None] * entering + local_here, end_here), entering)

    unused, entering = lax.scan(
        advance, (before[1], before[3]), (block_decay, local_state, first_float, end_float)
    )
    entering_low = entering.astype(jnp.bfloat16)
    carried_term = jnp.einsum(
        "ktn,khpn->kthp", c_blocks, entering_low, preferred_element_type=jnp.float32
    )
    lifting = jnp.exp(cumulative) * (doc_blocks[:, None, :] == first_docs[:, None, None]).astype(
        jnp.float32
    )
    carried_term = carried_term * jnp.transpose(lifting, (0, 2, 1))[..., None]
    result = block_term + carried_term + skip_gain[None, None, :, None] * x_blocks
    return result.astype(jnp.bfloat16).reshape(positions, head_count * attention_dimension)


def attention(queries, key_rows, values, log_scale, doc_ids):
    positions = queries.shape[0]
    q_local = log_scale.shape[0]
    kv_local = key_rows.shape[1] // HEAD_DIM
    ratio = q_local // kv_local
    q_places = lax.axis_index("ctx") * positions + jnp.arange(positions)
    grouped = queries.reshape(positions, kv_local, ratio, HEAD_DIM)
    stretch = (
        1.0 + log_scale[:, None] * jnp.log1p(q_places.astype(jnp.float32))[None, :]
    ) / math.sqrt(HEAD_DIM)
    stretch = stretch.reshape(kv_local, ratio, positions)

    def absorb(running, key_piece, value_piece, doc_piece, start):
        span = key_piece.shape[0]
        k_places = start + jnp.arange(span)
        allowed = (q_places[:, None] >= k_places[None, :]) & (
            doc_ids[:, None] == doc_piece.astype(jnp.int32)[None, :]
        )
        peak_old, totals, accum = running
        raw = jnp.einsum(
            "tjgd,sjd->jgts",
            grouped,
            key_piece.reshape(span, kv_local, HEAD_DIM),
            preferred_element_type=jnp.float32,
        )
        scores = jnp.where(allowed, raw * stretch[..., None], -1e30)
        peak_new = jnp.maximum(peak_old, jnp.max(scores, axis=3))
        probs = jnp.where(allowed, jnp.exp(scores - peak_new[..., None]), 0.0)
        rescale = jnp.exp(peak_old - peak_new)
        totals = totals * rescale + jnp.sum(probs, axis=3)
        mixed = jnp.einsum(
            "jgts,sjd->jgtd",
            probs.astype(jnp.bfloat16),
            value_piece.reshape(span, kv_local, HEAD_DIM),
            preferred_element_type=jnp.float32,
        )
        return (peak_new, totals, accum * rescale[..., None] + mixed)

    initial = (
        jnp.full((kv_local, ratio, positions), -1e30, jnp.float32),
        jnp.zeros((kv_local, ratio, positions), jnp.float32),
        jnp.zeros((kv_local, ratio, positions, HEAD_DIM), jnp.float32),
    )
    running = initial
    key_all = lax.all_gather(key_rows, "ctx", axis=0, tiled=True)
    value_all = lax.all_gather(values, "ctx", axis=0, tiled=True)
    doc_all = lax.all_gather(doc_ids.astype(jnp.bfloat16), "ctx", axis=0, tiled=True)
    span = key_all.shape[0]

    def one_part(current, part_index):
        offset = part_index * positions
        return (
            absorb(
                current,
                lax.dynamic_slice_in_dim(key_all, offset, positions, 0),
                lax.dynamic_slice_in_dim(value_all, offset, positions, 0),
                lax.dynamic_slice_in_dim(doc_all, offset, positions, 0),
                offset,
            ),
            None,
        )

    running, unused = lax.scan(one_part, running, jnp.arange(span // positions))
    peak_final, totals, accum = running
    mixed = accum / totals[..., None]
    return mixed.transpose(2, 0, 1, 3).reshape(positions, q_local * HEAD_DIM).astype(jnp.bfloat16)


def expert_layer(moe_in, expert_ids, route_weights, w_gate, w_up, w_down):
    positions = moe_in.shape[0]
    owners = lax.axis_size("mp")
    group = owners // HELD
    holder = lax.axis_index("mp") // group
    slots = 2 * positions // EXPERTS
    matches = expert_ids[:, :, None] == jnp.arange(HELD)[None, None, :]
    named = jnp.any(matches, axis=1)
    shares = jnp.sum(jnp.where(matches, route_weights[:, :, None], 0.0), axis=1)
    ranks = jnp.cumsum(named.astype(jnp.int32), axis=0) - 1
    placing = (named[:, :, None] & (ranks[:, :, None] == jnp.arange(slots)[None, None, :])).astype(
        jnp.bfloat16
    )
    own_place = lax.dynamic_index_in_dim(placing, holder, 1, keepdims=False)
    features = lax.all_gather(moe_in, "mp", axis=1, tiled=True)
    picked = jnp.einsum(
        "tc,td->cd", own_place, features, preferred_element_type=jnp.float32
    ).astype(jnp.bfloat16)
    gate_cols = w_gate[0]
    up_cols = w_up[0]
    down_rows = w_down[0]
    piece = lax.all_gather(picked, "ctx", axis=0, tiled=True)
    gate = jnp.dot(piece, gate_cols, preferred_element_type=jnp.float32)
    upward = jnp.dot(piece, up_cols, preferred_element_type=jnp.float32)
    hidden = (jax.nn.silu(gate) * upward).astype(jnp.bfloat16)
    summed = lax.psum_scatter(
        jnp.dot(hidden, down_rows, preferred_element_type=jnp.float32).astype(jnp.bfloat16),
        "ctx",
        scatter_dimension=0,
        tiled=True,
    ).astype(jnp.float32)
    own_share = lax.dynamic_index_in_dim(shares, holder, 1, keepdims=False)
    spread = (
        jnp.dot(own_place.astype(jnp.float32), summed, precision=lax.Precision.HIGHEST)
        * own_share[:, None]
    )
    return lax.psum_scatter(spread.astype(jnp.bfloat16), "mp", scatter_dimension=1, tiled=True)


def on_device(
    ssd_x,
    ssd_b,
    ssd_c,
    dt_steps,
    decay_rate,
    skip_gain,
    doc_ids,
    queries,
    key_rows,
    values,
    log_scale,
    moe_in,
    expert_ids,
    route_weights,
    w_gate,
    w_up,
    w_down,
):
    ssd_out = ssd_layer(ssd_x, ssd_b, ssd_c, dt_steps, decay_rate, skip_gain, doc_ids)
    attn_out = attention(queries, key_rows, values, log_scale, doc_ids)
    moe_out = expert_layer(moe_in, expert_ids, route_weights, w_gate, w_up, w_down)
    return (ssd_out, attn_out, moe_out)


def solution(mesh):
    in_specs = (
        P("ctx", "mp"),
        P("ctx", None),
        P("ctx", None),
        P("mp", "ctx"),
        P("mp"),
        P("mp"),
        P("ctx"),
        P("ctx", "mp"),
        P("ctx", "mp"),
        P("ctx", "mp"),
        P("mp"),
        P("ctx", "mp"),
        P("ctx", None),
        P("ctx", None),
        P("mp", None, "ctx"),
        P("mp", None, "ctx"),
        P("mp", "ctx", None),
    )
    out_specs = (P("ctx", "mp"), P("ctx", "mp"), P("ctx", "mp"))
    return jax.shard_map(
        on_device, mesh=mesh, in_specs=in_specs, out_specs=out_specs, check_vma=False
    )
```

profile of v0, /device:TPU:32, one launch (start us, length us, event | category | flops | bytes accessed | tf_op | source)
XLA Modules:
  0.0 456.7 jit_solution(7970416720867537943)
XLA Ops:
  10.4 33.5 %all-gather.15.cloned.1.call-done = bf16[256,8192]{1,0:T(8,128)(2,1)} async-done(((bf16[256,1024]{1,0:T(8,128)(2,1)}), bf16[256,8192]{1,0:T(8,128)(2,1)}) %all-gather.15.cloned.1.call-update) | async-done | bytes 4194320 | tf_op jit(solution)/shard_map/all_gather | solution.py:206
  43.8 3.8 convolution_convert_fusion.1
  49.0 69.4 %all-gather.17.cloned.1.call-done = bf16[512,8192]{1,0:T(8,128)(2,1)} async-done(((bf16[32,8192]{1,0:T(8,128)(2,1)}), bf16[512,8192]{1,0:T(8,128)(2,1)}) %all-gather.17.cloned.1.call-update) | async-done | bytes 8388624 | tf_op jit(solution)/shard_map/all_gather | solution.py:213
  118.4 9.0 %fusion.39 = f32[512,384]{1,0:T(8,128)S(1)} fusion(bf16[512,8192]{1,0:T(8,128)(2,1)} %all-gather.17.cloned.1.call-done, bf16[1,8192,384]{2,1,0:T(8,128)(2,1)} %param.39), kind=kOutput, calls=%fused_computation.68 | convolution fusion | flops 3221225472 | bytes 15466496 | tf_op jit(solution)/shard_map/dot_general | solution.py:214
  127.5 7.5 %fusion.48 = bf16[512,384]{1,0:T(8,128)(2,1)S(1)} fusion(bf16[512,8192]{1,0:T(8,128)(2,1)S(1)} %copy-done.14, bf16[1,8192,384]{2,1,0:T(8,128)(2,1)} %param.40, f32[512,384]{1,0:T(8,128)S(1)} %fusion.39), kind=kOutput, calls=%fused_computation.78 | convolution fusion | flops 3222405120 | bytes 15859712 | tf_op jit(solution)/shard_map/dot_general | solution.py:215
  135.0 6.7 %convolution_convert_fusion = bf16[512,8192]{1,0:T(8,128)(2,1)} fusion(bf16[512,384]{1,0:T(8,128)(2,1)S(1)} %fusion.48, bf16[1,384,8192]{2,1,0:T(8,128)(2,1)S(1)} %copy-done.15), kind=kOutput, calls=%fused_computation.61 | convolution fusion | flops 3225419776 | bytes 15073280 | tf_op jit(solution)/shard_map/dot_general | solution.py:218
  145.8 2.3 fusion.51
  148.1 8.2 %while.63 = (s32[]{:T(128)}, f32[8]{0:T(128)S(1)}, f32[8,256,128]{2,1,0:T(8,128)S(1)}, f32[1]{0:T(128)}, f32[1]{0:T(128)}, /*index=5*/f32[2,8]{1,0:T(2,128)S(1)}...) while((s32[]{:T(128)}, f32[8]{0:T(128)S(1)}, ...), condition=%wide.region_2.3_spmd.clone, body=%wide.region_1.2_spmd.clone.sunk | while | flops 786477 | bytes 3146148 | solution.py:97
  160.9 33.5 %all-reduce.3 = (bf16[128]{0:T(256)(128)(2,1)S(1)}, bf16[16]{0:T(256)(128)(2,1)S(1)}, bf16[16]{0:T(256)(128)(2,1)S(1)}) all-reduce(bf16[128]{0:T(256)(128)(2,1)S(1)} %dynamic-update-slice, bf16[16]{0:T(256)(128)(2,1)S(1)} %dynamic-update-slice.1, bf16[16]{0:T(256)(128)(2,1)S(1)} %dynamic-update-slice.2), channel_id=3, replica_groups=mesh['ctx'=16,'mp'=8] {'ctx'}, use_global_device_ids=true, to_apply=%add | all-reduce | flops 160 | bytes 640
  196.9 26.1 %all-gather.4 = bf16[16,1,256]{2,1,0:T(2,128)(2,1)S(1)} all-gather(bf16[1,1,256]{2,1,0:T(2,128)(2,1)S(1)} %reshape.212), channel_id=1, replica_groups=mesh['ctx'=16,'mp'=8] {'ctx'}, dimensions={0}, use_global_device_ids=true | all-gather | bytes 8704 | tf_op jit(solution)/shard_map/all_gather | solution.py:170
  223.3 110.9 %while.65 = (s32[]{:T(128)}, f32[1,8,256]{2,1,0:T(8,128)S(1)}, f32[1,8,256]{2,1,0:T(8,128)S(1)}, f32[1,8,256,128]{3,2,1,0:T(8,128)}, s32[16]{0:T(128)S(1)}, /*in...) while((s32[]{:T(128)}, f32[1,8,256]{2,1,0:T(8,128)S(1)}, ...), condition=%wide.region_10.11_spmd.clone, body=%wide.region_7.10_spmd.clone.sunk | while | flops 276253440 | bytes 9478935 | solution.py:186
  226.6 2.7 fusion.107
  233.1 3.2 fusion.107
  240.1 3.1 fusion.107
  247.0 3.2 fusion.107
  254.0 3.2 fusion.107
  261.0 3.2 fusion.107
  268.0 3.2 fusion.107
  275.0 3.1 fusion.107
  281.9 3.1 fusion.107
  288.8 3.2 fusion.107
  295.8 3.1 fusion.107
  302.7 3.1 fusion.107
  309.6 3.1 fusion.107
  316.6 3.2 fusion.107
  323.5 3.1 fusion.107
  330.5 3.1 fusion.107
  334.2 4.3 fusion.35
  341.3 25.6 %all-gather.19.cloned.1.call-done = bf16[128,256,128]{2,1,0:T(8,128)(2,1)} async-done(((bf16[8,256,128]{2,1,0:T(8,128)(2,1)}), bf16[128,256,128]{2,1,0:T(8,128)(2,1)}) %all-gather.19.cloned.1.call-update) | async-done | bytes 8388624 | tf_op jit(solution)/shard_map/all_gather | solution.py:17
  367.0 72.0 %while.64 = (s32[]{:T(128)}, f32[8,256,128]{2,1,0:T(8,128)S(1)}, f32[1]{0:T(128)}, s32[]{:T(128)}, bf16[16,8,256,128]{3,2,1,0:T(8,128)(2,1)}, /*index=5*/bf16[16...) while((s32[]{:T(128)}, f32[8,256,128]{2,1,0:T(8,128)S(1)}, ...), condition=%wide.region_4.5_spmd.clone, body=%wide.region_3.4_spmd.clone.sunk | while | flops 1310749 | bytes 2621756 | solution.py:34
  439.0 6.1 %while.62 = (s32[]{:T(128)}, f32[8,256,128]{2,1,0:T(8,128)S(1)}, f32[1]{0:T(128)}, bf16[2,8,256,128]{3,2,1,0:T(8,128)(2,1)}, f32[2,8]{1,0:T(2,128)S(1)}, /*index...) while((s32[]{:T(128)}, f32[8,256,128]{2,1,0:T(8,128)S(1)}, ...), condition=%wide.region_6.7_spmd, body=%wide.region_5.6_spmd.sunk | while | flops 1048580 | bytes 5244147 | solution.py:109
  445.1 1.7 fusion.79
  (336 shorter events, 107.9 us)
Async XLA Ops:
  7.2 138.7 %copy-start = (bf16[256,128]{1,0:T(8,128)(2,1)S(1)}, bf16[256,128]{1,0:T(8,128)(2,1)}, u32[]{:S(2)}) copy-start(bf16[256,128]{1,0:T(8,128)(2,1)} %param.26) | copy-start | bytes 196612
  7.2 36.7 %all-gather.15.cloned.1.call-start = ((), (), s32[]{:S(2)}) async-start(), calls=%async_computation.4 | async-start | bytes 4718592 | tf_op jit(solution)/shard_map/all_gather | solution.py:206
  7.9 110.5 %all-gather.17.cloned.1.call-start = ((), (), s32[]{:S(2)}) async-start(), calls=%async_computation.5 | async-start | bytes 8912896 | tf_op jit(solution)/shard_map/all_gather | solution.py:213
  47.6 175.6 %all-gather.11.cloned.1.call-start = ((), (), s32[]{:S(2)}) async-start(), calls=%async_computation.2 | async-start | bytes 1114112 | tf_op jit(solution)/shard_map/all_gather | solution.py:168
  48.4 174.9 %all-gather.13.cloned.1.call-start = ((), (), s32[]{:S(2)}) async-start(), calls=%async_computation.3 | async-start | bytes 1114112 | tf_op jit(solution)/shard_map/all_gather | solution.py:169
  49.0 285.2 %reduce-scatter.3.cloned.1.call-start = ((), (), s32[]{:S(2)}) async-start(), calls=%async_computation.6 | async-start | bytes 8912896 | tf_op jit(solution)/shard_map/reduce_scatter | solution.py:217
  118.4 9.0 %copy-start.14 = (bf16[512,8192]{1,0:T(8,128)(2,1)S(1)}, bf16[512,8192]{1,0:T(8,128)(2,1)}, u32[]{:S(2)}) copy-start(bf16[512,8192]{1,0:T(8,128)(2,1)} %all-gather.17.cloned.1.call-done) | copy-start | bytes 25165828
  127.5 7.5 %copy-start.15 = (bf16[1,384,8192]{2,1,0:T(8,128)(2,1)S(1)}, bf16[1,384,8192]{2,1,0:T(8,128)(2,1)}, u32[]{:S(2)}) copy-start(bf16[1,384,8192]{2,1,0:T(8,128)(2,1)} %param.41) | copy-start | bytes 18874372
  141.7 1.2 copy-start.6
  141.8 2.5 copy-start.8
  141.8 2.8 copy-start.10
  141.8 2.8 copy-start.13
  141.8 225.2 %all-gather.19.cloned.1.call-start = ((), (), s32[]{:S(2)}) async-start(), calls=%async_computation.8 | async-start | bytes 8912896 | tf_op jit(solution)/shard_map/all_gather | solution.py:17
  156.3 1.5 copy-start.2
  156.3 1.6 copy-start.17
  156.3 38.3 %copy-start.11 = (s32[256,2]{0,1:T(2,128)S(1)}, s32[256,2]{0,1:T(2,128)}, u32[]{:S(2)}) copy-start(s32[256,2]{0,1:T(2,128)} %param.37) | copy-start | bytes 6148
  156.3 38.3 %copy-start.12 = (f32[256,2]{0,1:T(2,128)S(1)}, f32[256,2]{0,1:T(2,128)}, u32[]{:S(2)}) copy-start(f32[256,2]{0,1:T(2,128)} %param.38) | copy-start | bytes 6148
  156.3 66.7 %copy-start.7 = (bf16[256,128]{1,0:T(8,128)(2,1)S(1)}, bf16[256,128]{1,0:T(8,128)(2,1)}, u32[]{:S(2)}) copy-start(bf16[256,128]{1,0:T(8,128)(2,1)} %param.27) | copy-start | bytes 196612
  156.4 67.0 %copy-start.9 = (f32[8]{0:T(128)S(1)}, f32[8]{0:T(128)}, u32[]{:S(2)}) copy-start(f32[8]{0:T(128)} %param.35) | copy-start | bytes 100
  157.3 292.6 %reduce-scatter.5.cloned.1.call-start = ((), (), s32[]{:S(2)}) async-start(), calls=%async_computation.7 | async-start | bytes 4718592 | tf_op jit(solution)/shard_map/reduce_scatter | solution.py:228
  338.5 1.2 copy-start.5
  367.0 72.0 %copy-start.3 = (f32[2,8,256,128]{3,2,1,0:T(8,128)S(1)}, f32[2,8,256,128]{3,2,1,0:T(8,128)}, u32[]{:S(2)}) copy-start(f32[2,8,256,128]{3,2,1,0:T(8,128)} %copy-done.2) | copy-start | bytes 6291460
  445.1 1.8 copy-start.4
  445.1 1.8 copy-start.16
  446.9 2.9 copy-start.1
Sparse Core Ops, SparseCore 0:
  9.7 34.0 all-gather.14
  47.8 70.6 all-gather.16
  120.6 42.2 all-gather.10
  164.9 42.1 all-gather.12
  210.3 84.5 reduce-scatter.2
  296.9 70.0 all-gather.18
  370.0 37.6 reduce-scatter.4
where the time goes:
time: 461 us; the launch traced here: 457 us
  waiting for transfers between devices  131 us (28%)
  matrix products  111 us (24%)
  loops' own time  60.2 us (13%)
  blocking collectives  59.6 us (13%)
  other arithmetic  44 us (10%)
  local copies, waits for them, and re-layouts  35.7 us (8%)
  between operations  15.3 us (3%)
    all_gather x1, waiting for transfers between devices, expert_layer(): piece = lax.all_gather(picked, 'ctx', axis=0, tiled=True)  69.4 us
    dot_general x16, matrix products, absorb(): jnp.einsum('jgts,sjd->jgtd', probs.astype(jnp.bfloat16), value_piece.resh...  49.9 us
    another operation x1, loops' own time, prefix(): return lax.fori_loop(0, count, lap, start)  39 us
    unnamed x1, blocking collectives  33.5 us
    all_gather x1, waiting for transfers between devices, expert_layer(): features = lax.all_gather(moe_in, 'mp', axis=1, tiled=True)  33.5 us
    all_gather x1, blocking collectives, attention(): lax.all_gather(doc_ids.astype(jnp.bfloat16), 'ctx', axis=0, tiled=True)  26.1 us
    all_gather x1, waiting for transfers between devices, prefix(): lax.all_gather(part.astype(kind), axis)  25.6 us
    dot_general x16, matrix products, absorb(): jnp.einsum('tjgd,sjd->jgts', grouped, key_piece.reshape(span, kv_local, H...  24.7 us
  transfers between devices with their start and end apart: 7, of which 3 were waited for; matrix products, arithmetic and copies ran while one was open for 40% of the time, Pallas kernels for 0%

commit v1 on v0

v1 whole, which is shorter than its diff:
```python
import math

import jax
import jax.numpy as jnp
from jax import lax
from jax.experimental import pallas as pl
from jax.experimental.pallas import tpu as pltpu
from jax.sharding import PartitionSpec as P

HEAD_DIM = 128
HELD = 4
SEG = 128
CAP = 32
WINDOW = 8
LOG2E = math.log2(math.e)
MESH = pl.DeviceIdType.MESH
F32 = jnp.float32
BF16 = jnp.bfloat16
HIGH = lax.Precision.HIGHEST


def dot(a, b, precision=None):
    return jnp.dot(a, b, preferred_element_type=F32, precision=precision)


def dot_nt(a, b, precision=None):
    return lax.dot_general(
        a, b, (((1,), (1,)), ((), ())), preferred_element_type=F32, precision=precision
    )


def iota(shape, dim):
    return lax.broadcasted_iota(jnp.int32, shape, dim)


def kernel(
    x_ref, b_ref, c_ref, ld_ref, skip_ref, docr_ref, docc_ref, q_ref, kv_ref, st_ref,
    moe_ref, ids_ref, rw_ref, wg_ref, wu_ref, wd_ref,
    ssd_out, attn_out, moe_out,
    wgu, wd, xs, pk, ptt, share, pl_land, l1, l2, qs, l3, l4, rx, fin, gu, hid,
    kv, sb, sl, en, er, t0s, ys, m_s, l_s, acc_s,
    w_sem, own_sem,
    xa_s, xa_r, sm_s, sm_r, bg_s, bg_r, bf_s, bf_r, cx_s, cx_r,
    cd_s, cd_r, ra_s, ra_r, rb_s, rb_r, xb_s, xb_r,
    kv_s, kv_r, sa_s, sa_r, se_s, se_r,
):
    c = lax.axis_index("ctx")
    m = lax.axis_index("mp")
    z, y = c // 4, c % 4
    x, g = m // 2, m % 2
    sib = {"ctx": c, "mp": x * 2 + (1 - g)}

    def zy(zz, yy):
        return {"ctx": (zz % 4) * 4 + yy % 4, "mp": m}

    def xdev(xx):
        return {"ctx": c, "mp": (xx % 4) * 2 + g}

    def ctx(cc):
        return {"ctx": cc % 16, "mp": m}

    def remote(src, dst, s, r, dev):
        return pltpu.make_async_remote_copy(
            src_ref=src, dst_ref=dst, send_sem=s, recv_sem=r, device_id=dev, device_id_type=MESH
        )

    loads = [
        pltpu.make_async_copy(wg_ref.at[0], wgu.at[:, pl.ds(0, 384)], w_sem.at[0]),
        pltpu.make_async_copy(wu_ref.at[0], wgu.at[:, pl.ds(384, 384)], w_sem.at[1]),
        pltpu.make_async_copy(wd_ref.at[0], wd, w_sem.at[2]),
    ]
    for load in loads:
        load.start()

    bar = pltpu.get_barrier_semaphore()
    for k in range(1, 16):
        pl.semaphore_signal(bar, inc=1, device_id=ctx(c + k), device_id_type=MESH)
    for k in range(1, 4):
        pl.semaphore_signal(bar, inc=1, device_id=xdev(x + k), device_id_type=MESH)
    pl.semaphore_signal(bar, inc=1, device_id=sib, device_id_type=MESH)

    expert = iota((8, 256), 0)
    ids0, ids1 = ids_ref[0:1, :], ids_ref[1:2, :]
    named = ((ids0 == expert) | (ids1 == expert)).astype(F32)
    weight = jnp.where(ids0 == expert, rw_ref[0:1, :], 0.0) + jnp.where(
        ids1 == expert, rw_ref[1:2, :], 0.0
    )
    upto = (iota((256, 256), 0) <= iota((256, 256), 1)).astype(BF16)
    rank = dot(named.astype(BF16), upto).astype(jnp.int32) - 1
    slot = iota((CAP, 256), 0)
    for e in range(HELD):
        place = jnp.where((rank[e : e + 1, :] == slot) & (named[e : e + 1, :] > 0.0), 1.0, 0.0)
        pk[e] = dot(place.astype(BF16), moe_ref[...]).astype(BF16)
        share[pl.ds(e * CAP, CAP), :] = jnp.broadcast_to(
            jnp.sum(place * weight[e : e + 1, :], axis=1, keepdims=True), (CAP, 128)
        )
        ptt[pl.ds(e * CAP, CAP), :] = place

    pl.semaphore_wait(bar, 19)

    xa = []
    for k in range(1, 4):
        cp = remote(
            pk.at[(x + k) % 4], xs.at[g, x, z, y], xa_s.at[k - 1], xa_r.at[k - 1], xdev(x + k)
        )
        cp.start()
        xa.append(cp)
    own = pltpu.make_async_copy(pk.at[x], xs.at[g, x, z, y], own_sem.at[0])
    own.start()
    kv0 = pltpu.make_async_copy(kv_ref, kv.at[0], own_sem.at[1])
    kv0.start()

    low = iota((SEG, SEG), 0) >= iota((SEG, SEG), 1)
    tri = low.astype(F32)
    cum_r, cum_c, inner, linked, bt = [], [], [], [], []
    for k in range(2):
        rows = slice(k * SEG, (k + 1) * SEG)
        ld = ld_ref[:, rows]
        cum_r.append(dot_nt(ld, tri, HIGH))
        cum_c.append(dot_nt(tri, ld, HIGH))
        inner.append(dot_nt(c_ref[rows, :], b_ref[rows, :]))
        linked.append((docc_ref[rows, :] == docr_ref[0:1, rows]) & low)
        bt.append(b_ref[rows, :].astype(F32).T)
    first = [docr_ref[:, k * SEG : k * SEG + 1] for k in range(2)]
    last = [docr_ref[:, k * SEG + SEG - 1 : (k + 1) * SEG] for k in range(2)]
    dec = [
        jnp.exp(cum_r[k][:, SEG - 1 : SEG]) * (first[k] == last[k]).astype(F32) for k in range(2)
    ]
    tail = [
        jnp.where(
            docr_ref[:, k * SEG : (k + 1) * SEG] == last[k],
            jnp.exp(cum_r[k][:, SEG - 1 : SEG] - cum_r[k]),
            0.0,
        )
        for k in range(2)
    ]
    lift = [
        jnp.exp(cum_c[k])
        * (docc_ref[k * SEG : (k + 1) * SEG, 0:8] == first[k][0:1, :]).astype(F32)
        for k in range(2)
    ]
    joined = (last[0] == first[1]).astype(F32)
    whole = dec[1] * joined * dec[0]

    def head_states(h):
        cols = slice(h * 256, (h + 1) * 256)
        locs = []
        for k in range(2):
            rows = slice(k * SEG, (k + 1) * SEG)
            xb = x_ref[rows, cols]
            locs.append(dot((bt[k] * tail[k][h : h + 1, :]).astype(BF16), xb))
        t0s[h] = locs[0]
        total = locs[1] + (dec[1] * joined)[h : h + 1, :] * locs[0]
        row = iota((16, 128), 0)
        w = jnp.broadcast_to(whole[h : h + 1, :], (16, 128))
        w_hi = w.astype(BF16).astype(F32)
        info = jnp.where(
            row == 0,
            w_hi,
            jnp.where(
                row == 1,
                w - w_hi,
                jnp.where(row == 2, first[0][0:1, :], last[1][0:1, :]),
            ),
        ).astype(BF16)
        for half in range(2):
            sb[2 * h + half, pl.ds(0, 128), :] = total[:, half * 128 : half * 128 + 128].astype(
                BF16
            )
            sb[2 * h + half, pl.ds(128, 16), :] = info

    def head_inside(h):
        cols = slice(h * 256, (h + 1) * 256)
        for k in range(2):
            rows = slice(k * SEG, (k + 1) * SEG)
            xb = x_ref[rows, cols]
            gap = cum_c[k][:, h : h + 1] - cum_r[k][h : h + 1, :]
            w = jnp.where(linked[k], inner[k] * jnp.exp(jnp.where(linked[k], gap, 0.0)), 0.0)
            ys[rows, cols] = dot(w.astype(BF16), xb) + skip_ref[h] * xb.astype(F32)

    for h in range(4):
        head_states(h)

    own.wait()
    for cp in xa:
        cp.wait()

    def xv(h, j, i, k):
        cols = pl.ds(2 * h, 2) if j is None else 2 * h + j
        return xs.at[g, cols, i % 4, k % 4] if h == 0 else xs.at[g, cols, k % 4, i % 4]

    big = (z, y)
    small = (y, z)

    def big_dev(h, d):
        return zy(z + d, y) if h == 0 else zy(z, y + d)

    def small_dev(h, d):
        return zy(z, y + d) if h == 0 else zy(z + d, y)

    order = (0, -1, 1, 2)

    def cp_small(h, d):
        v = xv(h, None, big[h], small[h])
        n = 0 if d == 1 else 1
        return remote(v, v, sm_s.at[h, n], sm_r.at[h, n], small_dev(h, d))

    def cp_small_fwd(h, d):
        n, j = (2, 0) if d == 1 else (3, 1)
        v = xv(h, j, big[h], small[h] - d + 4)
        return remote(v, v, sm_s.at[h, n], sm_r.at[h, n], small_dev(h, d))

    def cp_big(h, d, r):
        n = 0 if d == 1 else 1
        v = xv(h, None, big[h], small[h] + order[r] + 4)
        return remote(v, v, bg_s.at[h, n, r], bg_r.at[h, n, r], big_dev(h, d))

    def cp_big_fwd(h, d, r):
        n = 0 if d == 1 else 1
        v = xv(h, n, big[h] - d + 4, small[h] + order[r] + 4)
        return remote(v, v, bf_s.at[h, n, r], bf_r.at[h, n, r], big_dev(h, d))

    def cp_cross(h, d):
        i = (big[h] + d + 4) % 4
        cols = pl.ds(2 * h, 2)
        v = xs.at[g, cols, i] if h == 0 else xs.at[g, cols, :, i]
        return remote(v, v, cx_s.at[h, d % 4], cx_r.at[h, d % 4], sib)

    sends = []

    def go(cp):
        cp.start()
        sends.append(cp)

    for h in range(2):
        for d in (1, -1):
            go(cp_small(h, d))
    for h in range(2):
        for d in (1, -1):
            go(cp_big(h, d, 0))

    for h in range(4, 8):
        head_states(h)
    head_inside(0)

    for d, r in ((1, 1), (-1, 2)):
        for h in range(2):
            cp_small(h, d).wait_recv()
            go(cp_small_fwd(h, d))
            for e in (1, -1):
                go(cp_big(h, e, r))
    head_inside(1)
    for h in range(2):
        for d in (1, -1):
            cp_small_fwd(h, d).wait_recv()
        for e in (1, -1):
            go(cp_big(h, e, 3))
        go(cp_cross(h, 0))

    todo = [2, 3, 4, 5, 6, 7]
    for r in range(4):
        for h in range(2):
            for d in (1, -1):
                cp_big(h, d, r).wait_recv()
                go(cp_big_fwd(h, d, r))
        if todo:
            head_inside(todo.pop(0))
            head_inside(todo.pop(0))
    for h in range(2):
        go(cp_cross(h, -1))
        go(cp_cross(h, 1))

    def state_out(k):
        return remote(
            sb.at[(c + k) % 16], sl.at[c], sa_s.at[k], sa_r.at[k], ctx(c + k)
        )

    states = []
    for k in range(1, 16):
        cp = state_out(k)
        cp.start()
        states.append(cp)
    mine = pltpu.make_async_copy(sb.at[c], sl.at[c], own_sem.at[2])
    mine.start()

    kv0.wait()

    def key_out(k):
        return remote(kv.at[0], kv.at[k], kv_s.at[k], kv_r.at[k], ctx(c + k))

    for k in range(1, WINDOW + 1):

        @pl.when(c + k < 16)
        def _():
            key_out(k).start()

    for h in range(2):
        for r in range(4):
            for d in (1, -1):
                cp_big_fwd(h, d, r).wait_recv()
        go(cp_cross(h, 2))
    for cp in sends:
        cp.wait_send()

    def cross_in(h, d):
        i = (big[h] + d + 4) % 4
        cols = pl.ds(2 * h, 2)
        v = xs.at[1 - g, cols, i] if h == 0 else xs.at[1 - g, cols, :, i]
        return remote(v, v, cx_s.at[h, d % 4], cx_r.at[h, d % 4], sib)

    for h in range(2):
        for d in (0, -1, 1, 2):
            cross_in(h, d).wait_recv()
    for load in loads:
        load.wait()

    gu[...] = jnp.zeros_like(gu)

    def gate_up(i, carry):
        gg, xx = i // 4, i % 4
        block = pl.multiple_of((xx * 2 + gg) * 1024, 1024)
        gu[...] += dot(xs[gg, xx].reshape(512, 1024), wgu[pl.ds(block, 1024), :])
        return carry

    lax.fori_loop(0, 8, gate_up, 0)
    gate, up = gu[:, 0:384], gu[:, 384:768]
    hid[...] = (gate / (1.0 + jnp.exp(-gate)) * up).astype(BF16)

    ps, pa = xs.at[0], xs.at[1]

    def cp_down(xx):
        return remote(ps.at[xx], pl_land.at[xx], cd_s.at[xx], cd_r.at[xx], sib)

    for xx in range(4):

        def down_sib(n, carry):
            off = pl.multiple_of(n * 512, 512)
            col = pl.multiple_of((xx * 2 + 1 - g) * 1024 + n * 512, 512)
            r = dot(hid[...], wd[:, pl.ds(col, 512)])
            ps[xx, :, :, :, pl.ds(off, 512)] = r.astype(BF16).reshape(4, 4, CAP, 512)
            return carry

        lax.fori_loop(0, 2, down_sib, 0)
        cp_down(xx).start()

    def pv(h, j, i):
        return pa.at[2 * h + j, i % 4] if h == 0 else pa.at[2 * h + j, :, i % 4]

    def ra_first(h, j):
        d = 1 if j == 0 else -1
        return remote(
            pv(h, j, big[h] + 2), l1.at[h, j], ra_s.at[h, j], ra_r.at[h, j], big_dev(h, d)
        )

    def ra_block(h, j, d):
        n = 0 if d == 1 else 1
        return remote(
            pv(h, j, big[h] + d + 4),
            l2.at[h, n, j],
            ra_s.at[h, 2 + 2 * n + j],
            ra_r.at[h, 2 + 2 * n + j],
            big_dev(h, d),
        )

    for xx in range(4):
        cp_down(xx).wait_recv()

        def down_own(n, carry):
            off = pl.multiple_of(n * 512, 512)
            col = pl.multiple_of((xx * 2 + g) * 1024 + n * 512, 512)
            r = dot(hid[...], wd[:, pl.ds(col, 512)])
            r = r.reshape(4, 4, CAP, 512) + pl_land[xx, :, :, :, pl.ds(off, 512)].astype(F32)
            pa[xx, :, :, :, pl.ds(off, 512)] = r.astype(BF16)
            return carry

        lax.fori_loop(0, 2, down_own, 0)
        h, j = xx // 2, xx % 2
        ra_first(h, j).start()
        ra_block(h, j, -1 if j == 0 else 1).start()

    m_s[...] = jnp.full_like(m_s, -1e30)
    l_s[...] = jnp.zeros_like(l_s)
    acc_s[...] = jnp.zeros_like(acc_s)

    def absorb(k, diagonal):
        keys = kv[k, pl.ds(0, 256), :]
        vals = kv[k, pl.ds(256, 256), :]
        docs = kv[k, pl.ds(512, 16), :].astype(F32)
        doc_row = jnp.concatenate([docs[0:1, :], docs[1:2, :]], axis=1)
        docc = docc_ref[...]
        allowed = jnp.concatenate([docc, docc], axis=1) == doc_row
        if diagonal:
            allowed = allowed & (iota((256, 256), 0) >= iota((256, 256), 1))
        bias = jnp.where(allowed, 0.0, -1e30)
        for h in range(8):
            s = dot_nt(q_ref[:, h * 128 : h * 128 + 128], keys) + bias
            st = st_ref[:, h : h + 1]
            old = m_s[h][:, 0:1]
            new = jnp.maximum(old, jnp.max(s, axis=1, keepdims=True))
            p = jnp.exp2((s - new) * st)
            fade = jnp.exp2((old - new) * st)
            l_s[h] = l_s[h] * fade + jnp.sum(p, axis=1, keepdims=True)
            acc_s[h] = acc_s[h] * fade + dot(p.astype(BF16), vals)
            m_s[h] = jnp.broadcast_to(new, (256, 128))

    def absorb_range(lo, hi):
        def body(k, carry):
            remote(kv.at[0], kv.at[k], kv_s.at[k], kv_r.at[k], ctx(c + k)).wait_recv()
            absorb(k, False)
            return carry

        lax.fori_loop(lo, jnp.maximum(jnp.minimum(c + 1, hi), lo), body, 0)

    absorb(0, True)
    absorb_range(1, 2)

    for h in range(2):
        ra_first(h, 0).wait_recv()
        v = pv(h, 0, big[h] + 1)
        v[...] = (v[...].astype(F32) + l1[h, 0].astype(F32)).astype(BF16)
        ra_block(h, 0, 1).start()
        ra_first(h, 1).wait_recv()
        v = pv(h, 1, big[h] + 3)
        v[...] = (v[...].astype(F32) + l1[h, 1].astype(F32)).astype(BF16)
        ra_block(h, 1, -1).start()

    mine.wait()

    def scan(i, carry):
        state, before = carry

        @pl.when(i != c)
        def _():
            k = (c - i + 16) % 16
            remote(
                sb.at[c], sl.at[i], sa_s.at[k], sa_r.at[k], ctx(c + 1)
            ).wait_recv()

        info = sl[i, pl.ds(128, 16), :].astype(F32)
        entering = jnp.where(before == info[2:3, :], state, 0.0)
        en[i] = entering.astype(BF16)
        state = (info[0:1, :] + info[1:2, :]) * entering + sl[i, pl.ds(0, 128), :].astype(F32)
        return state, info[3:4, :]

    lax.fori_loop(
        0, 16, scan, (jnp.zeros((128, 128), F32), jnp.full((1, 128), -1.0, F32))
    )

    def state_back(k):
        return remote(en.at[(c + k) % 16], er.at[c], se_s.at[k], se_r.at[k], ctx(c + k))

    backs = []
    for k in range(1, 16):
        cp = state_back(k)
        cp.start()
        backs.append(cp)
    mine_back = pltpu.make_async_copy(en.at[c], er.at[c], own_sem.at[3])
    mine_back.start()

    absorb_range(2, 6)

    def rb_first(h, j):
        d = 1 if j == 0 else -1
        return remote(
            qs.at[h, j, (small[h] + 2) % 4],
            l3.at[h, j],
            rb_s.at[h, j],
            rb_r.at[h, j],
            small_dev(h, d),
        )

    def rb_block(h, j, d):
        n = 0 if d == 1 else 1
        return remote(
            qs.at[h, j, (small[h] + d + 4) % 4],
            l4.at[h, n, j],
            rb_s.at[h, 2 + 2 * n + j],
            rb_r.at[h, 2 + 2 * n + j],
            small_dev(h, d),
        )

    for h in range(2):
        for j in range(2):
            for d in (1, -1):
                ra_block(h, j, d).wait_recv()
            qs[h, j] = (
                pv(h, j, big[h])[...].astype(F32)
                + l2[h, 0, j].astype(F32)
                + l2[h, 1, j].astype(F32)
            ).astype(BF16)
            rb_first(h, j).start()
            rb_block(h, j, -1 if j == 0 else 1).start()

    absorb_range(6, 8)

    for h in range(2):
        for j, d in ((0, 1), (1, -1)):
            rb_first(h, j).wait_recv()
            v = qs.at[h, j, (small[h] + d + 4) % 4]
            v[...] = (v[...].astype(F32) + l3[h, j].astype(F32)).astype(BF16)
            rb_block(h, j, d).start()

    absorb_range(8, 9)

    share_x = share[pl.ds(pl.multiple_of(x * CAP, CAP), CAP), 0:1]

    def x_back(k):
        return remote(
            rx.at[(x + k) % 4], fin.at[x], xb_s.at[k - 1], xb_r.at[k - 1], xdev(x + k)
        )

    for h in range(2):
        for j in range(2):
            for d in (1, -1):
                rb_block(h, j, d).wait_recv()
            total = (
                qs[h, j, small[h]].astype(F32)
                + l4[h, 0, j].astype(F32)
                + l4[h, 1, j].astype(F32)
            )
            rx[2 * h + j] = (total * share_x).astype(BF16)
    for k in range(1, 4):
        x_back(k).start()
    own_back = pltpu.make_async_copy(rx.at[x], fin.at[x], own_sem.at[4])
    own_back.start()

    for h in range(8):
        attn_out[:, h * 128 : h * 128 + 128] = (acc_s[h] / l_s[h]).astype(BF16)

    mine_back.wait()
    for cp in backs:
        cp.wait()
    for h in range(8):
        cols = slice(h * 256, (h + 1) * 256)
        e0 = jnp.concatenate([er[2 * h], er[2 * h + 1]], axis=1)
        e1 = (
            joined[h : h + 1, :] * (dec[0][h : h + 1, :] * e0.astype(F32) + t0s[h])
        ).astype(BF16)
        for k, e in ((0, e0), (1, e1)):
            rows = slice(k * SEG, (k + 1) * SEG)
            carried = dot(c_ref[rows, :], e)
            ssd_out[rows, cols] = (ys[rows, cols] + carried * lift[k][:, h : h + 1]).astype(BF16)

    own_back.wait()
    for k in range(1, 4):
        x_back(k).wait()
    moe_out[...] = dot(ptt[...].T.astype(BF16), fin[...].reshape(128, 1024)).astype(BF16)

    for cp in states:
        cp.wait_send()
    for xx in range(4):
        cp_down(xx).wait_send()
    for h in range(2):
        for j in range(2):
            ra_first(h, j).wait_send()
            rb_first(h, j).wait_send()
            for d in (1, -1):
                ra_block(h, j, d).wait_send()
                rb_block(h, j, d).wait_send()
    for k in range(1, WINDOW + 1):

        @pl.when(c + k < 16)
        def _():
            key_out(k).wait_send()


def on_device(
    ssd_x, ssd_b, ssd_c, dt_steps, decay_rate, skip_gain, doc_ids,
    queries, key_rows, values, log_scale,
    moe_in, expert_ids, route_weights, w_gate, w_up, w_down,
):
    positions = ssd_x.shape[0]
    log_decay = -(dt_steps * decay_rate[:, None])
    docs = doc_ids.astype(F32)
    docr = jnp.broadcast_to(docs[None, :], (8, positions))
    docc = jnp.broadcast_to(docs[:, None], (positions, 128))
    kv = jnp.concatenate(
        [
            key_rows,
            values,
            docs.astype(BF16).reshape(2, 128),
            jnp.zeros((30, 128), BF16),
        ],
        axis=0,
    )
    places = lax.axis_index("ctx") * positions + jnp.arange(positions)
    stretch = (
        (1.0 + log_scale[None, :] * jnp.log1p(places.astype(F32))[:, None])
        * (LOG2E / math.sqrt(HEAD_DIM))
    )
    vmem = pl.BlockSpec(memory_space=pltpu.VMEM)
    smem = pl.BlockSpec(memory_space=pltpu.SMEM)
    anyw = pl.BlockSpec(memory_space=pl.ANY)
    dma = pltpu.SemaphoreType.DMA
    return pl.pallas_call(
        kernel,
        out_shape=(
            jax.ShapeDtypeStruct((positions, 2048), BF16),
            jax.ShapeDtypeStruct((positions, 1024), BF16),
            jax.ShapeDtypeStruct((positions, 1024), BF16),
        ),
        in_specs=[vmem] * 4 + [smem] + [vmem] * 8 + [anyw] * 3,
        out_specs=(vmem, vmem, vmem),
        scratch_shapes=[
            pltpu.VMEM((8192, 768), BF16),
            pltpu.VMEM((384, 8192), BF16),
            pltpu.VMEM((2, 4, 4, 4, CAP, 1024), BF16),
            pltpu.VMEM((4, CAP, 1024), BF16),
            pltpu.VMEM((128, 256), F32),
            pltpu.VMEM((128, 128), F32),
            pltpu.VMEM((4, 4, 4, CAP, 1024), BF16),
            pltpu.VMEM((2, 2, 4, CAP, 1024), BF16),
            pltpu.VMEM((2, 2, 2, 4, CAP, 1024), BF16),
            pltpu.VMEM((2, 2, 4, CAP, 1024), BF16),
            pltpu.VMEM((2, 2, CAP, 1024), BF16),
            pltpu.VMEM((2, 2, 2, CAP, 1024), BF16),
            pltpu.VMEM((4, CAP, 1024), BF16),
            pltpu.VMEM((4, CAP, 1024), BF16),
            pltpu.VMEM((512, 768), F32),
            pltpu.VMEM((512, 384), BF16),
            pltpu.VMEM((WINDOW + 1, 544, 128), BF16),
            pltpu.VMEM((16, 144, 128), BF16),
            pltpu.VMEM((16, 144, 128), BF16),
            pltpu.VMEM((16, 128, 128), BF16),
            pltpu.VMEM((16, 128, 128), BF16),
            pltpu.VMEM((8, 128, 256), F32),
            pltpu.VMEM((256, 2048), F32),
            pltpu.VMEM((8, 256, 128), F32),
            pltpu.VMEM((8, 256, 128), F32),
            pltpu.VMEM((8, 256, 128), F32),
            dma((3,)),
            dma((5,)),
            dma((3,)), dma((3,)),
            dma((2, 4)), dma((2, 4)),
            dma((2, 2, 4)), dma((2, 2, 4)),
            dma((2, 2, 4)), dma((2, 2, 4)),
            dma((2, 4)), dma((2, 4)),
            dma((4,)), dma((4,)),
            dma((2, 6)), dma((2, 6)),
            dma((2, 6)), dma((2, 6)),
            dma((3,)), dma((3,)),
            dma((WINDOW + 1,)), dma((WINDOW + 1,)),
            dma((16,)), dma((16,)),
            dma((16,)), dma((16,)),
        ],
        compiler_params=pltpu.CompilerParams(
            collective_id=0, has_side_effects=True, vmem_limit_bytes=60 * 2**20
        ),
        name="layer_pair",
    )(
        ssd_x, ssd_b, ssd_c, log_decay, skip_gain, docr, docc, queries, kv, stretch,
        moe_in, expert_ids.T, route_weights.T, w_gate, w_up, w_down,
    )


def solution(mesh):
    in_specs = (
        P("ctx", "mp"),
        P("ctx", None),
        P("ctx", None),
        P("mp", "ctx"),
        P("mp"),
        P("mp"),
        P("ctx"),
        P("ctx", "mp"),
        P("ctx", "mp"),
        P("ctx", "mp"),
        P("mp"),
        P("ctx", "mp"),
        P("ctx", None),
        P("ctx", None),
        P("mp", None, "ctx"),
        P("mp", None, "ctx"),
        P("mp", "ctx", None),
    )
    out_specs = (P("ctx", "mp"), P("ctx", "mp"), P("ctx", "mp"))
    return jax.shard_map(
        on_device, mesh=mesh, in_specs=in_specs, out_specs=out_specs, check_vma=False
    )
```

time: 461 us -> 142 us (0.31)
  waiting for transfers between devices: 131 us -> 0 us
  Pallas kernels: 0 us -> 129 us
  matrix products: 111 us -> 0 us
  loops' own time: 60.2 us -> 0 us
  blocking collectives: 59.6 us -> 0 us
  other arithmetic: 44 us -> 5.13 us
  local copies, waits for them, and re-layouts: 35.7 us -> 7.47 us
  between operations: 15.3 us -> 0.66 us
    pallas_call x0 -> x1, Pallas kernels: none -> 129 us  [on_device(): pl.pallas_call(kernel, out_shape=(jax.ShapeDtypeStruct((positions, 2048),...]
    all_gather x5 -> x0, waiting for transfers between devices: 129 us -> none  [the longest x1 69.4 us: expert_layer(): piece = lax.all_gather(picked, 'ctx', axis=0, tiled=True)]
    dot_general x41 -> x0, matrix products: 111 us -> none  [the longest x16 49.9 us: absorb(): jnp.einsum('jgts,sjd->jgtd', probs.astype(jnp.bfloat16), value_piece.resh...]
    another operation x4 -> x0, loops' own time: 60.2 us -> none  [the longest x1 39 us: prefix(): return lax.fori_loop(0, count, lap, start)]
    unnamed x1 -> x0, blocking collectives: 33.5 us -> none
    all_gather x1 -> x0, blocking collectives: 26.1 us -> none  [attention(): lax.all_gather(doc_ids.astype(jnp.bfloat16), 'ctx', axis=0, tiled=True)]
    dynamic_slice x39 -> x0, local copies, waits for them, and re-layouts: 23 us -> none  [the longest x16 10.7 us: attention(): running, unused = lax.scan(one_part, running, jnp.arange(span // positions))]
    select_n x16 -> x0, other arithmetic: 23 us -> none  [lap(): return jax.tree.map(lambda a, b: jnp.where(reached, a, b), new, before)]
  transfers between devices with their start and end apart: 7 -> 0, of which waited for: 3 -> 0; matrix products, arithmetic and copies ran while one was open for 40% -> 0% of each run, Pallas kernels for 0% -> 0%
where the time goes in v1:
time: 142 us
  Pallas kernels  129 us (91%)
  local copies, waits for them, and re-layouts  7.47 us (5%)
  other arithmetic  5.13 us (4%)
    pallas_call x1, Pallas kernels, on_device(): pl.pallas_call(kernel, out_shape=(jax.ShapeDtypeStruct((positions, 2048),...  129 us
    unnamed x3, local copies, waits for them, and re-layouts  6.04 us

profile of v1, /device:TPU:32, one launch (start us, length us, event | category | flops | bytes accessed | tf_op | source)
XLA Modules:
  0.0 142.1 jit_solution(12344822117575823206)
XLA Ops:
  0.7 0.1 pad.3.clone
  0.7 0.7 convert_bitcast_fusion
  1.4 0.6 broadcast_in_dim.6.docr_ref
  2.0 1.4 multiply_negate_fusion.ld_ref
  3.4 0.8 broadcast_in_dim.7.docc_ref
  4.1 1.4 add_multiply_fusion.st_ref
  5.5 1.7 %maximum_maximum_fusion.kv_ref = bf16[544,128]{1,0:T(8,128)(2,1)} fusion(bf16[2,128]{1,0:T(2,128)(2,1)S(1)} %get-tuple-element.3, bf16[256,128]{1,0:T(8,128)(2,1)} %param.26, bf16[256,128]{1,0:T(8,128)(2,1)} %param.25, bf16[544]{0:T(1024)(128)(2,1)S(1)} %pad.3.clone), kind=kLoop, calls=%fused_computation | loop fusion | flops 557056 | bytes 271936 | tf_op jit(solution)/shard_map/concatenate | solution.py:577
  7.2 128.8 %layer_pair.1 = (bf16[256,2048]{1,0:T(8,128)(2,1)}, bf16[256,1024]{1,0:T(8,128)(2,1)}, bf16[256,1024]{1,0:T(8,128)(2,1)}) custom-call(bf16[256,2048]{1,0:T(8,128)(2,1)} %x_ref.1, bf16[256,128]{1,0:T(8,128)(2,1)} %b_ref.1, bf16[256,128]{1,0:T(8,128)(2,1)} %c_ref.1, f32[8,256]{1,0:T(8,128)} %multiply_negate_fusion.ld_ref, f32[8]{0:T(128)} %skip_ref.1, ...), custom_call_target="tpu_custom_call" | custom-call | tf_op jit(solution)/shard_map/layer_pair/pallas_call | solution.py:595
  136.0 2.3 %copy.24 = bf16[256,2048]{1,0:T(8,128)(2,1)} copy(bf16[256,2048]{1,0:T(8,128)(2,1)} %get-tuple-element.8) | data formatting | bytes 2097152
  138.3 1.9 %copy.25 = bf16[256,1024]{1,0:T(8,128)(2,1)} copy(bf16[256,1024]{1,0:T(8,128)(2,1)} %get-tuple-element.9) | data formatting | bytes 1048576
  140.2 1.9 %copy.26 = bf16[256,1024]{1,0:T(8,128)(2,1)} copy(bf16[256,1024]{1,0:T(8,128)(2,1)} %get-tuple-element.10) | data formatting | bytes 1048576
  (2 shorter events, 0.0 us)

commit v2 on v1

--- a/solution.py
+++ b/solution.py
@@ -11,7 +11,6 @@
 HELD = 4
 SEG = 128
 CAP = 32
-WINDOW = 8
 LOG2E = math.log2(math.e)
 MESH = pl.DeviceIdType.MESH
 F32 = jnp.float32
@@ -34,15 +33,16 @@
 
 
 def kernel(
-    x_ref, b_ref, c_ref, ld_ref, skip_ref, docr_ref, docc_ref, q_ref, kv_ref, st_ref,
+    x_hbm, b_ref, c_ref, dt_ref, rate_ref, skip_ref, doc_ref, q_hbm, key_ref, val_ref, scale_ref,
     moe_ref, ids_ref, rw_ref, wg_ref, wu_ref, wd_ref,
-    ssd_out, attn_out, moe_out,
+    ssd_hbm, attn_hbm, moe_hbm,
+    x_ref, q_ref, docr_ref, docc_ref, st_ref, ssd_out, attn_out, moe_out,
     wgu, wd, xs, pk, ptt, share, pl_land, l1, l2, qs, l3, l4, rx, fin, gu, hid,
-    kv, sb, sl, en, er, t0s, ys, m_s, l_s, acc_s,
+    ka, va, sb, sl, en, er, t0s, ys, m_s, l_s, acc_s,
     w_sem, own_sem,
     xa_s, xa_r, sm_s, sm_r, bg_s, bg_r, bf_s, bf_r, cx_s, cx_r,
     cd_s, cd_r, ra_s, ra_r, rb_s, rb_r, xb_s, xb_r,
-    kv_s, kv_r, sa_s, sa_r, se_s, se_r,
+    ks_s, ks_r, out_sem, sa_s, sa_r, se_s, se_r,
 ):
     c = lax.axis_index("ctx")
     m = lax.axis_index("mp")
@@ -69,7 +69,13 @@
         pltpu.make_async_copy(wu_ref.at[0], wgu.at[:, pl.ds(384, 384)], w_sem.at[1]),
         pltpu.make_async_copy(wd_ref.at[0], wd, w_sem.at[2]),
     ]
-    for load in loads:
+    heads_in = [
+        pltpu.make_async_copy(key_ref, ka.at[z, y, pl.ds(0, 256)], own_sem.at[1]),
+        pltpu.make_async_copy(val_ref, va.at[z, y], own_sem.at[5]),
+        pltpu.make_async_copy(x_hbm, x_ref, own_sem.at[6]),
+        pltpu.make_async_copy(q_hbm, q_ref, own_sem.at[7]),
+    ]
+    for load in heads_in + loads:
         load.start()
 
     bar = pltpu.get_barrier_semaphore()
@@ -78,6 +84,19 @@
     for k in range(1, 4):
         pl.semaphore_signal(bar, inc=1, device_id=xdev(x + k), device_id_type=MESH)
     pl.semaphore_signal(bar, inc=1, device_id=sib, device_id_type=MESH)
+
+    docs = doc_ref[...].astype(F32)
+    docr_ref[...] = jnp.broadcast_to(docs, (8, 256))
+    docc_ref[...] = jnp.broadcast_to(docs, (128, 256)).T
+    ka[z, y, pl.ds(256, 16), :] = jnp.where(
+        iota((16, 128), 0) == 0, docs[:, 0:128], docs[:, 128:256]
+    ).astype(BF16)
+    growth = jnp.log((c * 256 + 1 + iota((256, 128), 0)).astype(F32))
+    lane = iota((256, 128), 1)
+    slope = jnp.zeros((256, 128), F32)
+    for h in range(8):
+        slope = jnp.where(lane == h, scale_ref[h], slope)
+    st_ref[...] = (1.0 + slope * growth) * (LOG2E / math.sqrt(HEAD_DIM))
 
     expert = iota((8, 256), 0)
     ids0, ids1 = ids_ref[0:1, :], ids_ref[1:2, :]
@@ -107,15 +126,63 @@
         xa.append(cp)
     own = pltpu.make_async_copy(pk.at[x], xs.at[g, x, z, y], own_sem.at[0])
     own.start()
-    kv0 = pltpu.make_async_copy(kv_ref, kv.at[0], own_sem.at[1])
-    kv0.start()
+    big = (z, y)
+    small = (y, z)
+
+    def big_dev(h, d):
+        return zy(z + d, y) if h == 0 else zy(z, y + d)
+
+    def small_dev(h, d):
+        return zy(z, y + d) if h == 0 else zy(z + d, y)
+
+    key_rows = ((0, 144), (144, 128)), ((0, 128), (128, 128))
+
+    def kcp(h, n, i, k, j, dev):
+        arr = (ka, va)[h]
+        rows = pl.ds(*key_rows[h][j]) if j is not None else slice(None)
+        if k is None:
+            v = arr.at[i % 4, :, rows] if h == 0 else arr.at[:, i % 4, rows]
+        else:
+            v = arr.at[i % 4, k % 4, rows] if h == 0 else arr.at[k % 4, i % 4, rows]
+        return remote(v, v, ks_s.at[h, n], ks_r.at[h, n], dev)
+
+    def k_small(h, d):
+        return kcp(h, 0 if d == 1 else 1, big[h], small[h], None, small_dev(h, d))
+
+    def k_small_fwd(h, d):
+        n, j = (2, 0) if d == 1 else (3, 1)
+        return kcp(h, n, big[h], small[h] - d + 4, j, small_dev(h, d))
+
+    def k_big(h, d):
+        return kcp(h, 4 if d == 1 else 5, big[h], None, None, big_dev(h, d))
+
+    def k_big_fwd(h, d):
+        n, j = (6, 0) if d == 1 else (7, 1)
+        return kcp(h, n, big[h] - d + 4, None, j, big_dev(h, d))
+
+    sends = []
+    k_sends = []
+
+    def go(cp, kept=None):
+        cp.start()
+        (sends if kept is None else kept).append(cp)
+
+    heads_in[0].wait()
+    heads_in[1].wait()
+    for h in range(2):
+        for d in (1, -1):
+            go(k_small(h, d), k_sends)
+    heads_in[2].wait()
 
     low = iota((SEG, SEG), 0) >= iota((SEG, SEG), 1)
     tri = low.astype(F32)
     cum_r, cum_c, inner, linked, bt = [], [], [], [], []
+    rate = jnp.zeros((8, 1), F32)
+    for h in range(8):
+        rate = jnp.where(iota((8, 1), 0) == h, rate_ref[h], rate)
     for k in range(2):
         rows = slice(k * SEG, (k + 1) * SEG)
-        ld = ld_ref[:, rows]
+        ld = -(dt_ref[:, rows] * rate)
         cum_r.append(dot_nt(ld, tri, HIGH))
         cum_c.append(dot_nt(tri, ld, HIGH))
         inner.append(dot_nt(c_ref[rows, :], b_ref[rows, :]))
@@ -178,8 +245,17 @@
             w = jnp.where(linked[k], inner[k] * jnp.exp(jnp.where(linked[k], gap, 0.0)), 0.0)
             ys[rows, cols] = dot(w.astype(BF16), xb) + skip_ref[h] * xb.astype(F32)
 
-    for h in range(4):
+    for h in range(8):
         head_states(h)
+
+    def state_out(k):
+        return remote(sb.at[(c + k) % 16], sl.at[c], sa_s.at[k], sa_r.at[k], ctx(c + k))
+
+    states = []
+    for k in range(1, 16):
+        go(state_out(k), states)
+    mine = pltpu.make_async_copy(sb.at[c], sl.at[c], own_sem.at[2])
+    mine.start()
 
     own.wait()
     for cp in xa:
@@ -188,15 +264,6 @@
     def xv(h, j, i, k):
         cols = pl.ds(2 * h, 2) if j is None else 2 * h + j
         return xs.at[g, cols, i % 4, k % 4] if h == 0 else xs.at[g, cols, k % 4, i % 4]
-
-    big = (z, y)
-    small = (y, z)
-
-    def big_dev(h, d):
-        return zy(z + d, y) if h == 0 else zy(z, y + d)
-
-    def small_dev(h, d):
-        return zy(z, y + d) if h == 0 else zy(z + d, y)
 
     order = (0, -1, 1, 2)
 
@@ -226,166 +293,15 @@
         v = xs.at[g, cols, i] if h == 0 else xs.at[g, cols, :, i]
         return remote(v, v, cx_s.at[h, d % 4], cx_r.at[h, d % 4], sib)
 
-    sends = []
-
-    def go(cp):
-        cp.start()
-        sends.append(cp)
-
-    for h in range(2):
-        for d in (1, -1):
-            go(cp_small(h, d))
-    for h in range(2):
-        for d in (1, -1):
-            go(cp_big(h, d, 0))
-
-    for h in range(4, 8):
-        head_states(h)
-    head_inside(0)
-
-    for d, r in ((1, 1), (-1, 2)):
-        for h in range(2):
-            cp_small(h, d).wait_recv()
-            go(cp_small_fwd(h, d))
-            for e in (1, -1):
-                go(cp_big(h, e, r))
-    head_inside(1)
-    for h in range(2):
-        for d in (1, -1):
-            cp_small_fwd(h, d).wait_recv()
-        for e in (1, -1):
-            go(cp_big(h, e, 3))
-        go(cp_cross(h, 0))
-
-    todo = [2, 3, 4, 5, 6, 7]
-    for r in range(4):
-        for h in range(2):
-            for d in (1, -1):
-                cp_big(h, d, r).wait_recv()
-                go(cp_big_fwd(h, d, r))
-        if todo:
-            head_inside(todo.pop(0))
-            head_inside(todo.pop(0))
-    for h in range(2):
-        go(cp_cross(h, -1))
-        go(cp_cross(h, 1))
-
-    def state_out(k):
-        return remote(
-            sb.at[(c + k) % 16], sl.at[c], sa_s.at[k], sa_r.at[k], ctx(c + k)
-        )
-
-    states = []
-    for k in range(1, 16):
-        cp = state_out(k)
-        cp.start()
-        states.append(cp)
-    mine = pltpu.make_async_copy(sb.at[c], sl.at[c], own_sem.at[2])
-    mine.start()
-
-    kv0.wait()
-
-    def key_out(k):
-        return remote(kv.at[0], kv.at[k], kv_s.at[k], kv_r.at[k], ctx(c + k))
-
-    for k in range(1, WINDOW + 1):
-
-        @pl.when(c + k < 16)
-        def _():
-            key_out(k).start()
-
-    for h in range(2):
-        for r in range(4):
-            for d in (1, -1):
-                cp_big_fwd(h, d, r).wait_recv()
-        go(cp_cross(h, 2))
-    for cp in sends:
-        cp.wait_send()
-
-    def cross_in(h, d):
-        i = (big[h] + d + 4) % 4
-        cols = pl.ds(2 * h, 2)
-        v = xs.at[1 - g, cols, i] if h == 0 else xs.at[1 - g, cols, :, i]
-        return remote(v, v, cx_s.at[h, d % 4], cx_r.at[h, d % 4], sib)
-
-    for h in range(2):
-        for d in (0, -1, 1, 2):
-            cross_in(h, d).wait_recv()
-    for load in loads:
-        load.wait()
-
-    gu[...] = jnp.zeros_like(gu)
-
-    def gate_up(i, carry):
-        gg, xx = i // 4, i % 4
-        block = pl.multiple_of((xx * 2 + gg) * 1024, 1024)
-        gu[...] += dot(xs[gg, xx].reshape(512, 1024), wgu[pl.ds(block, 1024), :])
-        return carry
-
-    lax.fori_loop(0, 8, gate_up, 0)
-    gate, up = gu[:, 0:384], gu[:, 384:768]
-    hid[...] = (gate / (1.0 + jnp.exp(-gate)) * up).astype(BF16)
-
-    ps, pa = xs.at[0], xs.at[1]
-
-    def cp_down(xx):
-        return remote(ps.at[xx], pl_land.at[xx], cd_s.at[xx], cd_r.at[xx], sib)
-
-    for xx in range(4):
-
-        def down_sib(n, carry):
-            off = pl.multiple_of(n * 512, 512)
-            col = pl.multiple_of((xx * 2 + 1 - g) * 1024 + n * 512, 512)
-            r = dot(hid[...], wd[:, pl.ds(col, 512)])
-            ps[xx, :, :, :, pl.ds(off, 512)] = r.astype(BF16).reshape(4, 4, CAP, 512)
-            return carry
-
-        lax.fori_loop(0, 2, down_sib, 0)
-        cp_down(xx).start()
-
-    def pv(h, j, i):
-        return pa.at[2 * h + j, i % 4] if h == 0 else pa.at[2 * h + j, :, i % 4]
-
-    def ra_first(h, j):
-        d = 1 if j == 0 else -1
-        return remote(
-            pv(h, j, big[h] + 2), l1.at[h, j], ra_s.at[h, j], ra_r.at[h, j], big_dev(h, d)
-        )
-
-    def ra_block(h, j, d):
-        n = 0 if d == 1 else 1
-        return remote(
-            pv(h, j, big[h] + d + 4),
-            l2.at[h, n, j],
-            ra_s.at[h, 2 + 2 * n + j],
-            ra_r.at[h, 2 + 2 * n + j],
-            big_dev(h, d),
-        )
-
-    for xx in range(4):
-        cp_down(xx).wait_recv()
-
-        def down_own(n, carry):
-            off = pl.multiple_of(n * 512, 512)
-            col = pl.multiple_of((xx * 2 + g) * 1024 + n * 512, 512)
-            r = dot(hid[...], wd[:, pl.ds(col, 512)])
-            r = r.reshape(4, 4, CAP, 512) + pl_land[xx, :, :, :, pl.ds(off, 512)].astype(F32)
-            pa[xx, :, :, :, pl.ds(off, 512)] = r.astype(BF16)
-            return carry
-
-        lax.fori_loop(0, 2, down_own, 0)
-        h, j = xx // 2, xx % 2
-        ra_first(h, j).start()
-        ra_block(h, j, -1 if j == 0 else 1).start()
-
     m_s[...] = jnp.full_like(m_s, -1e30)
     l_s[...] = jnp.zeros_like(l_s)
     acc_s[...] = jnp.zeros_like(acc_s)
 
     def absorb(k, diagonal):
-        keys = kv[k, pl.ds(0, 256), :]
-        vals = kv[k, pl.ds(256, 256), :]
-        docs = kv[k, pl.ds(512, 16), :].astype(F32)
+        there = c - k
+        keys = ka[there // 4, there % 4, pl.ds(0, 256), :]
+        vals = va[there // 4, there % 4]
+        docs = ka[there // 4, there % 4, pl.ds(256, 16), :].astype(F32)
         doc_row = jnp.concatenate([docs[0:1, :], docs[1:2, :]], axis=1)
         docc = docc_ref[...]
         allowed = jnp.concatenate([docc, docc], axis=1) == doc_row
@@ -405,14 +321,190 @@
 
     def absorb_range(lo, hi):
         def body(k, carry):
-            remote(kv.at[0], kv.at[k], kv_s.at[k], kv_r.at[k], ctx(c + k)).wait_recv()
             absorb(k, False)
             return carry
 
         lax.fori_loop(lo, jnp.maximum(jnp.minimum(c + 1, hi), lo), body, 0)
 
+    for h in range(2):
+        for d in (1, -1):
+            go(cp_small(h, d))
+    for h in range(2):
+        for d in (1, -1):
+            go(cp_big(h, d, 0))
+
+    head_inside(0)
+    head_inside(1)
+
+    for d, r in ((1, 1), (-1, 2)):
+        for h in range(2):
+            cp_small(h, d).wait_recv()
+            go(cp_small_fwd(h, d))
+            for e in (1, -1):
+                go(cp_big(h, e, r))
+    for h in range(2):
+        for d in (1, -1):
+            k_small(h, d).wait_recv()
+            go(k_small_fwd(h, d), k_sends)
+    heads_in[3].wait()
     absorb(0, True)
-    absorb_range(1, 2)
+    for h in range(2):
+        for d in (1, -1):
+            cp_small_fwd(h, d).wait_recv()
+        for e in (1, -1):
+            go(cp_big(h, e, 3))
+        go(cp_cross(h, 0))
+
+    def pass_on(r):
+        for h in range(2):
+            for d in (1, -1):
+                cp_big(h, d, r).wait_recv()
+                go(cp_big_fwd(h, d, r))
+
+    head_inside(2)
+    pass_on(0)
+    for h in range(2):
+        for d in (1, -1):
+            k_small_fwd(h, d).wait_recv()
+    head_inside(3)
+    head_inside(4)
+    pass_on(1)
+    pass_on(2)
+    head_inside(5)
+    head_inside(6)
+    head_inside(7)
+    pass_on(3)
+    for h in range(2):
+        go(cp_cross(h, -1))
+        go(cp_cross(h, 1))
+    for h in range(2):
+        for d in (1, -1):
+            go(k_big(h, d), k_sends)
+    mine.wait()
+
+    def scan(i, carry):
+        state, before = carry
+
+        @pl.when(i != c)
+        def _():
+            k = (c - i + 16) % 16
+            remote(
+                sb.at[c], sl.at[i], sa_s.at[k], sa_r.at[k], ctx(c + 1)
+            ).wait_recv()
+
+        info = sl[i, pl.ds(128, 16), :].astype(F32)
+        entering = jnp.where(before == info[2:3, :], state, 0.0)
+        en[i] = entering.astype(BF16)
+        state = (info[0:1, :] + info[1:2, :]) * entering + sl[i, pl.ds(0, 128), :].astype(F32)
+        return state, info[3:4, :]
+
+    lax.fori_loop(
+        0, 16, scan, (jnp.zeros((128, 128), F32), jnp.full((1, 128), -1.0, F32))
+    )
+
+    def state_back(k):
+        return remote(en.at[(c + k) % 16], er.at[c], se_s.at[k], se_r.at[k], ctx(c + k))
+
+    backs = []
+    for k in range(1, 16):
+        go(state_back(k), backs)
+    mine_back = pltpu.make_async_copy(en.at[c], er.at[c], own_sem.at[3])
+    mine_back.start()
+
+    for h in range(2):
+        for r in range(4):
+            for d in (1, -1):
+                cp_big_fwd(h, d, r).wait_recv()
+        go(cp_cross(h, 2))
+    for cp in sends:
+        cp.wait_send()
+
+    def cross_in(h, d):
+        i = (big[h] + d + 4) % 4
+        cols = pl.ds(2 * h, 2)
+        v = xs.at[1 - g, cols, i] if h == 0 else xs.at[1 - g, cols, :, i]
+        return remote(v, v, cx_s.at[h, d % 4], cx_r.at[h, d % 4], sib)
+
+    for h in range(2):
+        for d in (0, -1, 1, 2):
+            cross_in(h, d).wait_recv()
+    for load in loads:
+        load.wait()
+
+    gu[...] = jnp.zeros_like(gu)
+
+    def gate_up(i, carry):
+        gg, xx = i // 4, i % 4
+        block = pl.multiple_of((xx * 2 + gg) * 1024, 1024)
+        gu[...] += dot(xs[gg, xx].reshape(512, 1024), wgu[pl.ds(block, 1024), :])
+        return carry
+
+    lax.fori_loop(0, 4, gate_up, 0)
+    for h in range(2):
+        for d in (1, -1):
+            k_big(h, d).wait_recv()
+            go(k_big_fwd(h, d), k_sends)
+    lax.fori_loop(4, 8, gate_up, 0)
+    gate, up = gu[:, 0:384], gu[:, 384:768]
+    hid[...] = (gate / (1.0 + jnp.exp(-gate)) * up).astype(BF16)
+
+    ps, pa = xs.at[0], xs.at[1]
+
+    def cp_down(xx):
+        return remote(ps.at[xx], pl_land.at[xx], cd_s.at[xx], cd_r.at[xx], sib)
+
+    for xx in (0, 2, 1, 3):
+
+        def down_sib(n, carry):
+            off = pl.multiple_of(n * 512, 512)
+            col = pl.multiple_of((xx * 2 + 1 - g) * 1024 + n * 512, 512)
+            r = dot(hid[...], wd[:, pl.ds(col, 512)])
+            ps[xx, :, :, :, pl.ds(off, 512)] = r.astype(BF16).reshape(4, 4, CAP, 512)
+            return carry
+
+        lax.fori_loop(0, 2, down_sib, 0)
+        cp_down(xx).start()
+
+    def pv(h, j, i):
+        return pa.at[2 * h + j, i % 4] if h == 0 else pa.at[2 * h + j, :, i % 4]
+
+    def ra_first(h, j):
+        d = 1 if j == 0 else -1
+        return remote(
+            pv(h, j, big[h] + 2), l1.at[h, j], ra_s.at[h, j], ra_r.at[h, j], big_dev(h, d)
+        )
+
+    def ra_block(h, j, d):
+        n = 0 if d == 1 else 1
+        return remote(
+            pv(h, j, big[h] + d + 4),
+            l2.at[h, n, j],
+            ra_s.at[h, 2 + 2 * n + j],
+            ra_r.at[h, 2 + 2 * n + j],
+            big_dev(h, d),
+        )
+
+    for xx in (0, 2, 1, 3):
+        cp_down(xx).wait_recv()
+
+        def down_own(n, carry):
+            off = pl.multiple_of(n * 512, 512)
+            col = pl.multiple_of((xx * 2 + g) * 1024 + n * 512, 512)
+            r = dot(hid[...], wd[:, pl.ds(col, 512)])
+            r = r.reshape(4, 4, CAP, 512) + pl_land[xx, :, :, :, pl.ds(off, 512)].astype(F32)
+            pa[xx, :, :, :, pl.ds(off, 512)] = r.astype(BF16)
+            return carry
+
+        lax.fori_loop(0, 2, down_own, 0)
+        h, j = xx // 2, xx % 2
+        ra_first(h, j).start()
+        ra_block(h, j, -1 if j == 0 else 1).start()
+
+
+    for h in range(2):
+        for d in (1, -1):
+            k_big_fwd(h, d).wait_recv()
+    absorb_range(1, 3)
 
     for h in range(2):
         ra_first(h, 0).wait_recv()
@@ -424,40 +516,7 @@
         v[...] = (v[...].astype(F32) + l1[h, 1].astype(F32)).astype(BF16)
         ra_block(h, 1, -1).start()
 
-    mine.wait()
-
-    def scan(i, carry):
-        state, before = carry
-
-        @pl.when(i != c)
-        def _():
-            k = (c - i + 16) % 16
-            remote(
-                sb.at[c], sl.at[i], sa_s.at[k], sa_r.at[k], ctx(c + 1)
-            ).wait_recv()
-
-        info = sl[i, pl.ds(128, 16), :].astype(F32)
-        entering = jnp.where(before == info[2:3, :], state, 0.0)
-        en[i] = entering.astype(BF16)
-        state = (info[0:1, :] + info[1:2, :]) * entering + sl[i, pl.ds(0, 128), :].astype(F32)
-        return state, info[3:4, :]
-
-    lax.fori_loop(
-        0, 16, scan, (jnp.zeros((128, 128), F32), jnp.full((1, 128), -1.0, F32))
-    )
-
-    def state_back(k):
-        return remote(en.at[(c + k) % 16], er.at[c], se_s.at[k], se_r.at[k], ctx(c + k))
-
-    backs = []
-    for k in range(1, 16):
-        cp = state_back(k)
-        cp.start()
-        backs.append(cp)
-    mine_back = pltpu.make_async_copy(en.at[c], er.at[c], own_sem.at[3])
-    mine_back.start()
-
-    absorb_range(2, 6)
+    absorb_range(3, 7)
 
     def rb_first(h, j):
         d = 1 if j == 0 else -1
@@ -491,7 +550,7 @@
             rb_first(h, j).start()
             rb_block(h, j, -1 if j == 0 else 1).start()
 
-    absorb_range(6, 8)
+    absorb_range(7, 8)
 
     for h in range(2):
         for j, d in ((0, 1), (1, -1)):
@@ -526,6 +585,8 @@
 
     for h in range(8):
         attn_out[:, h * 128 : h * 128 + 128] = (acc_s[h] / l_s[h]).astype(BF16)
+    attn_done = pltpu.make_async_copy(attn_out, attn_hbm, out_sem.at[0])
+    attn_done.start()
 
     mine_back.wait()
     for cp in backs:
@@ -541,11 +602,19 @@
             carried = dot(c_ref[rows, :], e)
             ssd_out[rows, cols] = (ys[rows, cols] + carried * lift[k][:, h : h + 1]).astype(BF16)
 
+    ssd_done = pltpu.make_async_copy(ssd_out, ssd_hbm, out_sem.at[1])
+    ssd_done.start()
+
     own_back.wait()
     for k in range(1, 4):
         x_back(k).wait()
     moe_out[...] = dot(ptt[...].T.astype(BF16), fin[...].reshape(128, 1024)).astype(BF16)
 
+    moe_done = pltpu.make_async_copy(moe_out, moe_hbm, out_sem.at[2])
+    moe_done.start()
+
+    for cp in k_sends:
+        cp.wait_send()
     for cp in states:
         cp.wait_send()
     for xx in range(4):
@@ -557,11 +626,30 @@
             for d in (1, -1):
                 ra_block(h, j, d).wait_send()
                 rb_block(h, j, d).wait_send()
-    for k in range(1, WINDOW + 1):
-
-        @pl.when(c + k < 16)
-        def _():
-            key_out(k).wait_send()
+    attn_done.wait()
+    ssd_done.wait()
+    moe_done.wait()
+
+
+def settle(*refs):
+    sources, results, held, sems = refs[0:3], refs[3:6], refs[6:9], refs[9]
+    parts = []
+    for i in range(3):
+        for p in range(2):
+            rows = pl.ds(p * 128, 128)
+            into = pltpu.make_async_copy(
+                sources[i].at[rows], held[i].at[rows], sems.at[0, i, p]
+            )
+            back = pltpu.make_async_copy(
+                held[i].at[rows], results[i].at[rows], sems.at[1, i, p]
+            )
+            into.start()
+            parts.append((into, back))
+    for into, back in parts:
+        into.wait()
+        back.start()
+    for into, back in parts:
+        back.wait()
 
 
 def on_device(
@@ -570,38 +658,31 @@
     moe_in, expert_ids, route_weights, w_gate, w_up, w_down,
 ):
     positions = ssd_x.shape[0]
-    log_decay = -(dt_steps * decay_rate[:, None])
-    docs = doc_ids.astype(F32)
-    docr = jnp.broadcast_to(docs[None, :], (8, positions))
-    docc = jnp.broadcast_to(docs[:, None], (positions, 128))
-    kv = jnp.concatenate(
-        [
-            key_rows,
-            values,
-            docs.astype(BF16).reshape(2, 128),
-            jnp.zeros((30, 128), BF16),
-        ],
-        axis=0,
-    )
-    places = lax.axis_index("ctx") * positions + jnp.arange(positions)
-    stretch = (
-        (1.0 + log_scale[None, :] * jnp.log1p(places.astype(F32))[:, None])
-        * (LOG2E / math.sqrt(HEAD_DIM))
-    )
     vmem = pl.BlockSpec(memory_space=pltpu.VMEM)
     smem = pl.BlockSpec(memory_space=pltpu.SMEM)
     anyw = pl.BlockSpec(memory_space=pl.ANY)
     dma = pltpu.SemaphoreType.DMA
-    return pl.pallas_call(
+    shapes = (
+        jax.ShapeDtypeStruct((positions, 2048), BF16),
+        jax.ShapeDtypeStruct((positions, 1024), BF16),
+        jax.ShapeDtypeStruct((positions, 1024), BF16),
+    )
+    made = pl.pallas_call(
         kernel,
-        out_shape=(
-            jax.ShapeDtypeStruct((positions, 2048), BF16),
-            jax.ShapeDtypeStruct((positions, 1024), BF16),
-            jax.ShapeDtypeStruct((positions, 1024), BF16),
-        ),
-        in_specs=[vmem] * 4 + [smem] + [vmem] * 8 + [anyw] * 3,
-        out_specs=(vmem, vmem, vmem),
+        out_shape=shapes,
+        in_specs=[anyw, vmem, vmem, vmem, smem, smem, vmem, anyw, anyw, anyw, smem]
+        + [vmem] * 3
+        + [anyw] * 3,
+        out_specs=(anyw, anyw, anyw),
         scratch_shapes=[
+            pltpu.VMEM((256, 2048), BF16),
+            pltpu.VMEM((256, 1024), BF16),
+            pltpu.VMEM((8, 256), F32),
+            pltpu.VMEM((256, 128), F32),
+            pltpu.VMEM((256, 128), F32),
+            pltpu.VMEM((256, 2048), BF16),
+            pltpu.VMEM((256, 1024), BF16),
+            pltpu.VMEM((256, 1024), BF16),
             pltpu.VMEM((8192, 768), BF16),
             pltpu.VMEM((384, 8192), BF16),
             pltpu.VMEM((2, 4, 4, 4, CAP, 1024), BF16),
@@ -618,7 +699,8 @@
             pltpu.VMEM((4, CAP, 1024), BF16),
             pltpu.VMEM((512, 768), F32),
             pltpu.VMEM((512, 384), BF16),
-            pltpu.VMEM((WINDOW + 1, 544, 128), BF16),
+            pltpu.VMEM((4, 4, 272, 128), BF16),
+            pltpu.VMEM((4, 4, 256, 128), BF16),
             pltpu.VMEM((16, 144, 128), BF16),
             pltpu.VMEM((16, 144, 128), BF16),
             pltpu.VMEM((16, 128, 128), BF16),
@@ -629,7 +711,7 @@
             pltpu.VMEM((8, 256, 128), F32),
             pltpu.VMEM((8, 256, 128), F32),
             dma((3,)),
-            dma((5,)),
+            dma((8,)),
             dma((3,)), dma((3,)),
             dma((2, 4)), dma((2, 4)),
             dma((2, 2, 4)), dma((2, 2, 4)),
@@ -639,7 +721,8 @@
             dma((2, 6)), dma((2, 6)),
             dma((2, 6)), dma((2, 6)),
             dma((3,)), dma((3,)),
-            dma((WINDOW + 1,)), dma((WINDOW + 1,)),
+            dma((2, 8)), dma((2, 8)),
+            dma((3,)),
             dma((16,)), dma((16,)),
             dma((16,)), dma((16,)),
         ],
@@ -648,9 +731,24 @@
         ),
         name="layer_pair",
     )(
-        ssd_x, ssd_b, ssd_c, log_decay, skip_gain, docr, docc, queries, kv, stretch,
+        ssd_x, ssd_b, ssd_c, dt_steps, decay_rate, skip_gain, doc_ids[None, :],
+        queries, key_rows, values, log_scale,
         moe_in, expert_ids.T, route_weights.T, w_gate, w_up, w_down,
     )
+    return pl.pallas_call(
+        settle,
+        out_shape=shapes,
+        in_specs=[anyw] * 3,
+        out_specs=(anyw, anyw, anyw),
+        scratch_shapes=[
+            pltpu.VMEM((256, 2048), BF16),
+            pltpu.VMEM((256, 1024), BF16),
+            pltpu.VMEM((256, 1024), BF16),
+            dma((2, 3, 2)),
+        ],
+        compiler_params=pltpu.CompilerParams(vmem_limit_bytes=60 * 2**20),
+        name="settle",
+    )(*made)
 
 
 def solution(mesh):

time: 142 us -> 111 us (0.78)
  Pallas kernels: 129 us -> 109 us
  local copies, waits for them, and re-layouts: 7.47 us -> 0 us
  other arithmetic: 5.13 us -> 0 us
    pallas_call x1 -> x2, Pallas kernels: 129 us -> 109 us  [the longest x1 106 us: on_device(): pl.pallas_call(kernel, out_shape=shapes, in_specs=[anyw, vmem, vmem, vmem...]
    unnamed x3 -> x0, local copies, waits for them, and re-layouts: 6.04 us -> none
    concatenate x1 -> x0, other arithmetic: 1.67 us -> none  [on_device(): jnp.concatenate([key_rows, values, docs.astype(BF16).reshape(2, 128), jnp...]
where the time goes in v2:
time: 111 us; the launch traced here: 110 us
  Pallas kernels  109 us (98%)
    pallas_call x1, Pallas kernels, on_device(): pl.pallas_call(kernel, out_shape=shapes, in_specs=[anyw, vmem, vmem, vmem...  106 us
    pallas_call x1, Pallas kernels, on_device(): pl.pallas_call(settle, out_shape=shapes, in_specs=[anyw] * 3, out_specs=(...  2.45 us

profile of v2, /device:TPU:32, one launch (start us, length us, event | category | flops | bytes accessed | tf_op | source)
XLA Modules:
  0.0 109.7 jit_solution(8351846315458880626)
XLA Ops:
  0.6 106.5 %layer_pair.1 = (bf16[256,2048]{1,0:T(8,128)(2,1)}, bf16[256,1024]{1,0:T(8,128)(2,1)}, bf16[256,1024]{1,0:T(8,128)(2,1)}) custom-call(bf16[256,2048]{1,0:T(8,128)(2,1)} %x_hbm.1, bf16[256,128]{1,0:T(8,128)(2,1)} %b_ref.1, bf16[256,128]{1,0:T(8,128)(2,1)} %c_ref.1, f32[8,256]{1,0:T(8,128)} %dt_ref.1, f32[8]{0:T(128)} %rate_ref.1, f32[8]{0:T(128)} %skip_ref.1, ...), custom_call_target="tpu_custom_call" | custom-call | tf_op jit(solution)/shard_map/layer_pair/pallas_call | solution.py:670
  107.1 2.5 %settle.1 = (bf16[256,2048]{1,0:T(8,128)(2,1)}, bf16[256,1024]{1,0:T(8,128)(2,1)}, bf16[256,1024]{1,0:T(8,128)(2,1)}) custom-call(bf16[256,2048]{1,0:T(8,128)(2,1)} %get-tuple-element.6.refs_0_, bf16[256,1024]{1,0:T(8,128)(2,1)} %get-tuple-element.7.refs_1_, bf16[256,1024]{1,0:T(8,128)(2,1)} %get-tuple-element.8.refs_2_), custom_call_target="tpu_custom_call" | custom-call | tf_op jit(solution)/shard_map/settle/pallas_call | solution.py:738

commit v3 on v2

--- a/solution.py
+++ b/solution.py
@@ -91,11 +91,10 @@
     ka[z, y, pl.ds(256, 16), :] = jnp.where(
         iota((16, 128), 0) == 0, docs[:, 0:128], docs[:, 128:256]
     ).astype(BF16)
-    growth = jnp.log((c * 256 + 1 + iota((256, 128), 0)).astype(F32))
-    lane = iota((256, 128), 1)
-    slope = jnp.zeros((256, 128), F32)
+    growth = jnp.log((c * 256 + 1 + iota((8, 256), 1)).astype(F32))
+    slope = jnp.zeros((8, 256), F32)
     for h in range(8):
-        slope = jnp.where(lane == h, scale_ref[h], slope)
+        slope = jnp.where(iota((8, 256), 0) == h, scale_ref[h], slope)
     st_ref[...] = (1.0 + slope * growth) * (LOG2E / math.sqrt(HEAD_DIM))
 
     expert = iota((8, 256), 0)
@@ -303,21 +302,22 @@
         vals = va[there // 4, there % 4]
         docs = ka[there // 4, there % 4, pl.ds(256, 16), :].astype(F32)
         doc_row = jnp.concatenate([docs[0:1, :], docs[1:2, :]], axis=1)
-        docc = docc_ref[...]
-        allowed = jnp.concatenate([docc, docc], axis=1) == doc_row
+        doc_col = jnp.broadcast_to(doc_row, (128, 256)).T
+        allowed = jnp.concatenate([doc_col, doc_col], axis=1) == docr_ref[0:1, :]
         if diagonal:
-            allowed = allowed & (iota((256, 256), 0) >= iota((256, 256), 1))
+            allowed = allowed & (iota((256, 256), 0) <= iota((256, 256), 1))
         bias = jnp.where(allowed, 0.0, -1e30)
+        vals_t = vals.astype(F32).T.astype(BF16)
         for h in range(8):
-            s = dot_nt(q_ref[:, h * 128 : h * 128 + 128], keys) + bias
-            st = st_ref[:, h : h + 1]
-            old = m_s[h][:, 0:1]
-            new = jnp.maximum(old, jnp.max(s, axis=1, keepdims=True))
+            s = dot_nt(keys, q_ref[:, h * 128 : h * 128 + 128]) + bias
+            st = st_ref[h : h + 1, :]
+            old = m_s[h : h + 1, :]
+            new = jnp.maximum(old, jnp.max(s, axis=0, keepdims=True))
             p = jnp.exp2((s - new) * st)
             fade = jnp.exp2((old - new) * st)
-            l_s[h] = l_s[h] * fade + jnp.sum(p, axis=1, keepdims=True)
-            acc_s[h] = acc_s[h] * fade + dot(p.astype(BF16), vals)
-            m_s[h] = jnp.broadcast_to(new, (256, 128))
+            l_s[h : h + 1, :] = l_s[h : h + 1, :] * fade + jnp.sum(p, axis=0, keepdims=True)
+            acc_s[h] = acc_s[h] * fade + dot(vals_t, p.astype(BF16))
+            m_s[h : h + 1, :] = new
 
     def absorb_range(lo, hi):
         def body(k, carry):
@@ -416,9 +416,21 @@
             for d in (1, -1):
                 cp_big_fwd(h, d, r).wait_recv()
         go(cp_cross(h, 2))
-    for cp in sends:
-        cp.wait_send()
-
+    for load in loads:
+        load.wait()
+    gu[...] = jnp.zeros_like(gu)
+
+    def gate_up(i, carry):
+        gg, xx = (i // 4 + g) % 2, i % 4
+        block = pl.multiple_of((xx * 2 + gg) * 1024, 1024)
+        gu[...] += dot(xs[gg, xx].reshape(512, 1024), wgu[pl.ds(block, 1024), :])
+        return carry
+
+    lax.fori_loop(0, 4, gate_up, 0)
+    for h in range(2):
+        for d in (1, -1):
+            k_big(h, d).wait_recv()
+            go(k_big_fwd(h, d), k_sends)
     def cross_in(h, d):
         i = (big[h] + d + 4) % 4
         cols = pl.ds(2 * h, 2)
@@ -428,26 +440,12 @@
     for h in range(2):
         for d in (0, -1, 1, 2):
             cross_in(h, d).wait_recv()
-    for load in loads:
-        load.wait()
-
-    gu[...] = jnp.zeros_like(gu)
-
-    def gate_up(i, carry):
-        gg, xx = i // 4, i % 4
-        block = pl.multiple_of((xx * 2 + gg) * 1024, 1024)
-        gu[...] += dot(xs[gg, xx].reshape(512, 1024), wgu[pl.ds(block, 1024), :])
-        return carry
-
-    lax.fori_loop(0, 4, gate_up, 0)
-    for h in range(2):
-        for d in (1, -1):
-            k_big(h, d).wait_recv()
-            go(k_big_fwd(h, d), k_sends)
     lax.fori_loop(4, 8, gate_up, 0)
     gate, up = gu[:, 0:384], gu[:, 384:768]
     hid[...] = (gate / (1.0 + jnp.exp(-gate)) * up).astype(BF16)
 
+    for cp in sends:
+        cp.wait_send()
     ps, pa = xs.at[0], xs.at[1]
 
     def cp_down(xx):
@@ -504,19 +502,19 @@
     for h in range(2):
         for d in (1, -1):
             k_big_fwd(h, d).wait_recv()
-    absorb_range(1, 3)
-
-    for h in range(2):
-        ra_first(h, 0).wait_recv()
-        v = pv(h, 0, big[h] + 1)
-        v[...] = (v[...].astype(F32) + l1[h, 0].astype(F32)).astype(BF16)
-        ra_block(h, 0, 1).start()
-        ra_first(h, 1).wait_recv()
-        v = pv(h, 1, big[h] + 3)
-        v[...] = (v[...].astype(F32) + l1[h, 1].astype(F32)).astype(BF16)
-        ra_block(h, 1, -1).start()
-
-    absorb_range(3, 7)
+    def add_first(h, j):
+        d = 1 if j == 0 else -1
+        ra_first(h, j).wait_recv()
+        v = pv(h, j, big[h] + d + 4)
+        v[...] = (v[...].astype(F32) + l1[h, j].astype(F32)).astype(BF16)
+        ra_block(h, j, d).start()
+
+    add_first(0, 0)
+    add_first(1, 0)
+    absorb_range(1, 4)
+    add_first(0, 1)
+    add_first(1, 1)
+    absorb_range(4, 7)
 
     def rb_first(h, j):
         d = 1 if j == 0 else -1
@@ -550,7 +548,8 @@
             rb_first(h, j).start()
             rb_block(h, j, -1 if j == 0 else 1).start()
 
-    absorb_range(7, 8)
+
+    absorb_range(7, 9)
 
     for h in range(2):
         for j, d in ((0, 1), (1, -1)):
@@ -559,7 +558,28 @@
             v[...] = (v[...].astype(F32) + l3[h, j].astype(F32)).astype(BF16)
             rb_block(h, j, d).start()
 
-    absorb_range(8, 9)
+    for h in range(8):
+        attn_out[:, h * 128 : h * 128 + 128] = (acc_s[h] / l_s[h : h + 1, :]).T.astype(BF16)
+    attn_done = pltpu.make_async_copy(attn_out, attn_hbm, out_sem.at[0])
+    attn_done.start()
+
+    mine_back.wait()
+    for cp in backs:
+        cp.wait()
+    for h in range(8):
+        cols = slice(h * 256, (h + 1) * 256)
+        e0 = jnp.concatenate([er[2 * h], er[2 * h + 1]], axis=1)
+        e1 = (
+            joined[h : h + 1, :] * (dec[0][h : h + 1, :] * e0.astype(F32) + t0s[h])
+        ).astype(BF16)
+        for k, e in ((0, e0), (1, e1)):
+            rows = slice(k * SEG, (k + 1) * SEG)
+            carried = dot(c_ref[rows, :], e)
+            ssd_out[rows, cols] = (ys[rows, cols] + carried * lift[k][:, h : h + 1]).astype(BF16)
+
+    ssd_done = pltpu.make_async_copy(ssd_out, ssd_hbm, out_sem.at[1])
+    ssd_done.start()
+
 
     share_x = share[pl.ds(pl.multiple_of(x * CAP, CAP), CAP), 0:1]
 
@@ -582,28 +602,6 @@
         x_back(k).start()
     own_back = pltpu.make_async_copy(rx.at[x], fin.at[x], own_sem.at[4])
     own_back.start()
-
-    for h in range(8):
-        attn_out[:, h * 128 : h * 128 + 128] = (acc_s[h] / l_s[h]).astype(BF16)
-    attn_done = pltpu.make_async_copy(attn_out, attn_hbm, out_sem.at[0])
-    attn_done.start()
-
-    mine_back.wait()
-    for cp in backs:
-        cp.wait()
-    for h in range(8):
-        cols = slice(h * 256, (h + 1) * 256)
-        e0 = jnp.concatenate([er[2 * h], er[2 * h + 1]], axis=1)
-        e1 = (
-            joined[h : h + 1, :] * (dec[0][h : h + 1, :] * e0.astype(F32) + t0s[h])
-        ).astype(BF16)
-        for k, e in ((0, e0), (1, e1)):
-            rows = slice(k * SEG, (k + 1) * SEG)
-            carried = dot(c_ref[rows, :], e)
-            ssd_out[rows, cols] = (ys[rows, cols] + carried * lift[k][:, h : h + 1]).astype(BF16)
-
-    ssd_done = pltpu.make_async_copy(ssd_out, ssd_hbm, out_sem.at[1])
-    ssd_done.start()
 
     own_back.wait()
     for k in range(1, 4):
@@ -679,7 +677,7 @@
             pltpu.VMEM((256, 1024), BF16),
             pltpu.VMEM((8, 256), F32),
             pltpu.VMEM((256, 128), F32),
-            pltpu.VMEM((256, 128), F32),
+            pltpu.VMEM((8, 256), F32),
             pltpu.VMEM((256, 2048), BF16),
             pltpu.VMEM((256, 1024), BF16),
             pltpu.VMEM((256, 1024), BF16),
@@ -707,9 +705,9 @@
             pltpu.VMEM((16, 128, 128), BF16),
             pltpu.VMEM((8, 128, 256), F32),
             pltpu.VMEM((256, 2048), F32),
-            pltpu.VMEM((8, 256, 128), F32),
-            pltpu.VMEM((8, 256, 128), F32),
-            pltpu.VMEM((8, 256, 128), F32),
+            pltpu.VMEM((8, 256), F32),
+            pltpu.VMEM((8, 256), F32),
+            pltpu.VMEM((8, 128, 256), F32),
             dma((3,)),
             dma((8,)),
             dma((3,)), dma((3,)),

time: 111 us -> 106 us (0.955)
  Pallas kernels: 109 us -> 103 us
    pallas_call x1, Pallas kernels: 106 us -> 101 us  [on_device(): pl.pallas_call(kernel, out_shape=shapes, in_specs=[anyw, vmem, vmem, vmem...]
where the time goes in v3:
time: 106 us; the launch traced here: 104 us
  Pallas kernels  103 us (97%)
    pallas_call x1, Pallas kernels, on_device(): pl.pallas_call(kernel, out_shape=shapes, in_specs=[anyw, vmem, vmem, vmem...  101 us
    pallas_call x1, Pallas kernels, on_device(): pl.pallas_call(settle, out_shape=shapes, in_specs=[anyw] * 3, out_specs=(...  2.45 us

profile of v3, /device:TPU:32, one launch (start us, length us, event | category | flops | bytes accessed | tf_op | source)
XLA Modules:
  0.0 104.1 jit_solution(16402412720266680021)
XLA Ops:
  0.6 100.9 %layer_pair.1 = (bf16[256,2048]{1,0:T(8,128)(2,1)}, bf16[256,1024]{1,0:T(8,128)(2,1)}, bf16[256,1024]{1,0:T(8,128)(2,1)}) custom-call(bf16[256,2048]{1,0:T(8,128)(2,1)} %x_hbm.1, bf16[256,128]{1,0:T(8,128)(2,1)} %b_ref.1, bf16[256,128]{1,0:T(8,128)(2,1)} %c_ref.1, f32[8,256]{1,0:T(8,128)} %dt_ref.1, f32[8]{0:T(128)} %rate_ref.1, f32[8]{0:T(128)} %skip_ref.1, ...), custom_call_target="tpu_custom_call" | custom-call | tf_op jit(solution)/shard_map/layer_pair/pallas_call | solution.py:668
  101.5 2.5 %settle.1 = (bf16[256,2048]{1,0:T(8,128)(2,1)}, bf16[256,1024]{1,0:T(8,128)(2,1)}, bf16[256,1024]{1,0:T(8,128)(2,1)}) custom-call(bf16[256,2048]{1,0:T(8,128)(2,1)} %get-tuple-element.6.refs_0_, bf16[256,1024]{1,0:T(8,128)(2,1)} %get-tuple-element.7.refs_1_, bf16[256,1024]{1,0:T(8,128)(2,1)} %get-tuple-element.8.refs_2_), custom_call_target="tpu_custom_call" | custom-call | tf_op jit(solution)/shard_map/settle/pallas_call | solution.py:736

commit v4 on v3

--- a/solution.py
+++ b/solution.py
@@ -496,7 +496,9 @@
         lax.fori_loop(0, 2, down_own, 0)
         h, j = xx // 2, xx % 2
         ra_first(h, j).start()
-        ra_block(h, j, -1 if j == 0 else 1).start()
+        if j == 1:
+            ra_block(h, 0, -1).start()
+            ra_block(h, 1, 1).start()
 
 
     for h in range(2):

time: 106 us -> 106 us (level)
  no operation moved by 1% of the time
where the time goes in v4:
time: 106 us; the launch traced here: 104 us
  Pallas kernels  103 us (97%)
    pallas_call x1, Pallas kernels, on_device(): pl.pallas_call(kernel, out_shape=shapes, in_specs=[anyw, vmem, vmem, vmem...  101 us
    pallas_call x1, Pallas kernels, on_device(): pl.pallas_call(settle, out_shape=shapes, in_specs=[anyw] * 3, out_specs=(...  2.45 us

profile of v4, /device:TPU:32, one launch (start us, length us, event | category | flops | bytes accessed | tf_op | source)
XLA Modules:
  0.0 104.1 jit_solution(5563538454105728092)
XLA Ops:
  0.6 100.9 %layer_pair.1 = (bf16[256,2048]{1,0:T(8,128)(2,1)}, bf16[256,1024]{1,0:T(8,128)(2,1)}, bf16[256,1024]{1,0:T(8,128)(2,1)}) custom-call(bf16[256,2048]{1,0:T(8,128)(2,1)} %x_hbm.1, bf16[256,128]{1,0:T(8,128)(2,1)} %b_ref.1, bf16[256,128]{1,0:T(8,128)(2,1)} %c_ref.1, f32[8,256]{1,0:T(8,128)} %dt_ref.1, f32[8]{0:T(128)} %rate_ref.1, f32[8]{0:T(128)} %skip_ref.1, ...), custom_call_target="tpu_custom_call" | custom-call | tf_op jit(solution)/shard_map/layer_pair/pallas_call | solution.py:670
  101.5 2.5 %settle.1 = (bf16[256,2048]{1,0:T(8,128)(2,1)}, bf16[256,1024]{1,0:T(8,128)(2,1)}, bf16[256,1024]{1,0:T(8,128)(2,1)}) custom-call(bf16[256,2048]{1,0:T(8,128)(2,1)} %get-tuple-element.6.refs_0_, bf16[256,1024]{1,0:T(8,128)(2,1)} %get-tuple-element.7.refs_1_, bf16[256,1024]{1,0:T(8,128)(2,1)} %get-tuple-element.8.refs_2_), custom_call_target="tpu_custom_call" | custom-call | tf_op jit(solution)/shard_map/settle/pallas_call | solution.py:738
